TPU v7x, 32 devices: a whole 2x2x4 slice. The times are simulated.
32 devices in a mesh: head: 4 (over y, x), blk: 8 (over z, core).
Axes of the slice: x: 2, y: 2, z: 4, core: 2. Of those that a mesh axis runs over, the one named last changes fastest.
Arguments:
- inputs: bfloat16 [8192, 1024], P(('blk', 'head')), may hold values from -6 to 6
- query_weight: bfloat16 [1024, 1024], P(('head', 'blk')), may hold values from -0.1875 to 0.1875
- key_weight: bfloat16 [1024, 512], P(('head', 'blk')), may hold values from -0.1875 to 0.1875
- value_weight: bfloat16 [1024, 512], P(('head', 'blk')), may hold values from -0.1875 to 0.1875
- mixing_weight: bfloat16 [1024, 1024], P(('head', 'blk')), may hold values from -1.5 to 1.5
- gate_weight: bfloat16 [1024, 4608], P(('head', 'blk')), may hold values from -0.1875 to 0.1875
- up_weight: bfloat16 [1024, 4608], P(('head', 'blk')), may hold values from -0.1875 to 0.1875
- down_weight: bfloat16 [4608, 1024], P(('head', 'blk')), may hold values from -0.09375 to 0.09375
- attention_gain: bfloat16 [1024], P(('head', 'blk')), may hold values from 0.5 to 1.5
- feedforward_gain: bfloat16 [1024], P(('head', 'blk')), may hold values from 0.5 to 1.5
- query_gain: bfloat16 [64], replicated, may hold values from 1 to 2
- key_gain: bfloat16 [64], replicated, may hold values from 1 to 2
- cotangent: bfloat16 [8192, 1024], P(('blk', 'head')), may hold values from -6 to 6
Outputs:
- output: bfloat16 [8192, 1024], P(('blk', 'head'))
- input_gradient: bfloat16 [8192, 1024], P(('blk', 'head'))
- query_gradient: float32 [1024, 1024], P(('head', 'blk'))
- key_gradient: float32 [1024, 512], P(('head', 'blk'))
- value_gradient: float32 [1024, 512], P(('head', 'blk'))
- mixing_gradient: float32 [1024, 1024], P(('head', 'blk'))
- gate_gradient: float32 [1024, 4608], P(('head', 'blk'))
- up_gradient: float32 [1024, 4608], P(('head', 'blk'))
- down_gradient: float32 [4608, 1024], P(('head', 'blk'))
- attention_gain_gradient: float32 [1024], P(('head', 'blk'))
- feedforward_gain_gradient: float32 [1024], P(('head', 'blk'))
- query_gain_gradient: float32 [64], replicated
- key_gain_gradient: float32 [64], replicated
All inputs are finite; a program needn't handle non-finite values.
Results may differ from a plain program's by a relative error of at most 0.035.
Values may be sent and summed in bfloat16 or wider, within the bound.
No kernel may reach another device: no remote copies, remote signals or barrier semaphores. Data moves between devices by JAX's collectives and lax.ppermute only.
A program may use at most 192 MiB of HBM per device.

v0:
```python
import math

import jax
import jax.numpy as jnp
from jax import lax
from jax.sharding import PartitionSpec as P

HQ = 16
KV = 8
HD = 64


EPSILON = 1e-05
ROPE_BASE = 1000000.0
NEGATIVE = -1e30


def from_behind(shard, axis, by):
    count = lax.axis_size(axis)
    pairs = [(i, i + by) for i in range(count) if 0 <= i + by < count]
    return lax.ppermute(shard, axis, pairs)


def shifted(value, axis, steps):
    count = lax.axis_size(axis)
    pairs = [(source, (source + steps) % count) for source in range(count)]
    return lax.ppermute(value, axis, pairs)


def rms_scale(values, gain_row):
    return (
        values * lax.rsqrt(jnp.mean(values * values, axis=-1, keepdims=True) + EPSILON) * gain_row
    )


def rope_tables(positions, head_size):
    half_size = head_size // 2
    frequency = jnp.exp(
        jnp.arange(half_size).astype(jnp.float32) * (-2.0 * math.log(ROPE_BASE) / head_size)
    )
    angles = positions.astype(jnp.float32)[:, None] * frequency[None, :]
    return (jnp.cos(angles), jnp.sin(angles))


def rotate(values, cosine_table, sine_table):
    half_size = values.shape[-1] // 2
    first_half = values[..., :half_size]
    second_half = values[..., half_size:]
    cosine_wide = cosine_table[:, None, :]
    sine_wide = sine_table[:, None, :]
    return jnp.concatenate(
        [
            first_half * cosine_wide - second_half * sine_wide,
            second_half * cosine_wide + first_half * sine_wide,
        ],
        axis=-1,
    )


def head_norm_rope(raw, gain_row, cosine_table, sine_table):
    row_count = raw.shape[0]
    shaped = raw.reshape(row_count, -1, HD)
    return rotate(rms_scale(shaped, gain_row), cosine_table, sine_table).reshape(row_count, -1)


def swish_product(gate_value, up_value):
    return gate_value * jax.nn.sigmoid(gate_value) * up_value


def gather_tokens(values):
    return lax.all_gather(values, "head", axis=0, tiled=True)


def sum_tokens(values):
    return lax.psum_scatter(
        values.astype(jnp.bfloat16), "head", scatter_dimension=0, tiled=True
    ).astype(jnp.float32)


def per_device(
    inputs,
    query_weight,
    key_weight,
    value_weight,
    mixing_weight,
    gate_weight,
    up_weight,
    down_weight,
    attention_gain,
    feedforward_gain,
    query_gain,
    key_gain,
    cotangent,
):
    head_count = lax.axis_size("head")
    block_count = lax.axis_size("blk")
    block_index = lax.axis_index("blk")
    tok_rows = inputs.shape[0]
    span_rows = tok_rows * head_count
    group_size = HQ // KV
    shared_heads = KV // head_count
    score_scale = HD ** (-0.5)
    first_query = block_index * span_rows
    query_place = first_query + jnp.arange(span_rows, dtype=jnp.int32)
    key_offsets = jnp.arange(span_rows, dtype=jnp.int32)
    inputs_float = inputs.astype(jnp.float32)
    (
        rows_query,
        rows_key,
        rows_value,
        rows_mixing,
        rows_gate,
        rows_up,
        rows_down,
        rows_norm_attention,
        rows_norm_feed,
    ) = (
        lax.all_gather(query_weight, "blk", axis=0, tiled=True),
        lax.all_gather(key_weight, "blk", axis=0, tiled=True),
        lax.all_gather(value_weight, "blk", axis=0, tiled=True),
        lax.all_gather(mixing_weight, "blk", axis=0, tiled=True),
        lax.all_gather(gate_weight, "blk", axis=0, tiled=True),
        lax.all_gather(up_weight, "blk", axis=0, tiled=True),
        lax.all_gather(down_weight, "blk", axis=0, tiled=True),
        lax.all_gather(attention_gain, "blk", axis=0, tiled=True),
        lax.all_gather(feedforward_gain, "blk", axis=0, tiled=True),
    )
    tile_attention = jnp.broadcast_to(
        rows_norm_attention[:, None], (rows_norm_attention.shape[0], head_count)
    )
    tile_feed = jnp.broadcast_to(rows_norm_feed[:, None], (rows_norm_feed.shape[0], head_count))
    full_query, full_key, full_value, full_gate, full_up, tile_attention, tile_feed = (
        lax.all_to_all(rows_query, "head", split_axis=1, concat_axis=0, tiled=True),
        lax.all_to_all(rows_key, "head", split_axis=1, concat_axis=0, tiled=True),
        lax.all_to_all(rows_value, "head", split_axis=1, concat_axis=0, tiled=True),
        lax.all_to_all(rows_gate, "head", split_axis=1, concat_axis=0, tiled=True),
        lax.all_to_all(rows_up, "head", split_axis=1, concat_axis=0, tiled=True),
        lax.all_to_all(tile_attention, "head", split_axis=1, concat_axis=0, tiled=True),
        lax.all_to_all(tile_feed, "head", split_axis=1, concat_axis=0, tiled=True),
    )
    full_norm_attention = tile_attention[:, 0]
    full_norm_feed = tile_feed[:, 0]
    cosine_table, sine_table = rope_tables(query_place, HD)

    def rotated_heads(raw, gain_row):
        return head_norm_rope(raw, gain_row, cosine_table, sine_table)

    normed, normed_back = jax.vjp(rms_scale, inputs_float, full_norm_attention.astype(jnp.float32))
    normed_low = normed.astype(jnp.bfloat16)
    normed_rows = gather_tokens(normed_low)
    query_raw = jnp.dot(normed_rows, full_query, preferred_element_type=jnp.float32)
    key_raw = jnp.dot(normed_rows, full_key, preferred_element_type=jnp.float32)
    value_low = jnp.dot(normed_rows, full_value, preferred_element_type=jnp.float32).astype(
        jnp.bfloat16
    )
    query_final, query_back = jax.vjp(rotated_heads, query_raw, query_gain.astype(jnp.float32))
    key_final, key_back = jax.vjp(rotated_heads, key_raw, key_gain.astype(jnp.float32))
    query_heads = query_final.astype(jnp.bfloat16)
    key_heads = key_final.astype(jnp.bfloat16)
    query_grouped = query_heads.reshape(span_rows, shared_heads, group_size, HD)
    start_state = (
        jnp.full((shared_heads, group_size, span_rows), NEGATIVE, jnp.float32),
        jnp.zeros((shared_heads, group_size, span_rows), jnp.float32),
        jnp.zeros((shared_heads, group_size, span_rows, HD), jnp.float32),
    )
    running = start_state
    key_piece = lax.all_gather(key_heads, "blk", axis=0, tiled=True)
    value_piece = lax.all_gather(value_low, "blk", axis=0, tiled=True)
    piece_blocks = key_piece.shape[0] // span_rows
    key_blocks = key_piece.reshape(piece_blocks, span_rows, shared_heads, HD)
    value_blocks = value_piece.reshape(piece_blocks, span_rows, shared_heads, HD)
    block_starts = span_rows * jnp.arange(piece_blocks, dtype=jnp.int32)

    def visit_block(state_now, block_data):
        key_block, value_block, block_start = block_data

        def update(state_in):
            run_max, run_sum, run_acc = state_in
            scores = (
                jnp.einsum(
                    "qkgd,skd->kgqs", query_grouped, key_block, preferred_element_type=jnp.float32
                )
                * score_scale
            )
            allowed = (block_start + key_offsets)[None, :] <= query_place[:, None]
            scores = jnp.where(allowed, scores, NEGATIVE)
            new_max = jnp.maximum(run_max, jnp.max(scores, axis=-1))
            factor = jnp.exp(run_max - new_max)
            exponent = jnp.exp(scores - new_max[..., None])
            new_sum = run_sum * factor + jnp.sum(exponent, axis=-1)
            new_acc = run_acc * factor[..., None] + jnp.einsum(
                "kgqs,skd->kgqd",
                exponent.astype(jnp.bfloat16),
                value_block,
                preferred_element_type=jnp.float32,
            )
            return (new_max, new_sum, new_acc)

        return (
            lax.cond(block_start <= first_query, update, lambda state_in: state_in, state_now),
            None,
        )

    running, unused = lax.scan(visit_block, running, (key_blocks, value_blocks, block_starts))
    run_max, run_sum, run_acc = running
    out_grouped = run_acc / run_sum[..., None]
    log_total = run_max + jnp.log(run_sum)
    out_rows = out_grouped.transpose(2, 0, 1, 3).reshape(span_rows, -1).astype(jnp.bfloat16)
    hidden = inputs_float + sum_tokens(
        jnp.dot(out_rows, rows_mixing, preferred_element_type=jnp.float32)
    )
    normed_ffn, normed_ffn_back = jax.vjp(rms_scale, hidden, full_norm_feed.astype(jnp.float32))
    normed_ffn_low = normed_ffn.astype(jnp.bfloat16)
    ffn_rows = gather_tokens(normed_ffn_low)
    cot_rows = gather_tokens(cotangent)
    gate_value = jnp.dot(ffn_rows, full_gate, preferred_element_type=jnp.float32)
    up_value = jnp.dot(ffn_rows, full_up, preferred_element_type=jnp.float32)
    activation, activation_back = jax.vjp(swish_product, gate_value, up_value)
    activation_low = activation.astype(jnp.bfloat16)
    down_term = jnp.dot(activation_low, rows_down, preferred_element_type=jnp.float32)
    down_term = sum_tokens(down_term)
    output = (hidden + down_term).astype(jnp.bfloat16)
    down_grad = jnp.dot(activation_low.T, cot_rows, preferred_element_type=jnp.float32)
    activation_grad = jnp.dot(cot_rows, rows_down.T, preferred_element_type=jnp.float32).astype(
        jnp.bfloat16
    )
    gate_grad_float, up_grad_float = activation_back(activation_grad.astype(jnp.float32))
    gate_grad_low = gate_grad_float.astype(jnp.bfloat16)
    up_grad_low = up_grad_float.astype(jnp.bfloat16)
    gate_grad = jnp.dot(ffn_rows.T, gate_grad_low, preferred_element_type=jnp.float32)
    up_grad = jnp.dot(ffn_rows.T, up_grad_low, preferred_element_type=jnp.float32)
    normed_ffn_grad = jnp.dot(
        gate_grad_low, full_gate.T, preferred_element_type=jnp.float32
    ) + jnp.dot(up_grad_low, full_up.T, preferred_element_type=jnp.float32)
    normed_ffn_grad = sum_tokens(normed_ffn_grad)
    hidden_part, feed_gain_grad = normed_ffn_back(normed_ffn_grad)
    hidden_grad = cotangent.astype(jnp.float32) + hidden_part
    hidden_low = hidden_grad.astype(jnp.bfloat16)
    hidden_rows = gather_tokens(hidden_low)
    mixing_grad = jnp.dot(out_rows.T, hidden_rows, preferred_element_type=jnp.float32)
    mixture_grad = jnp.dot(hidden_rows, rows_mixing.T, preferred_element_type=jnp.float32).astype(
        jnp.bfloat16
    )
    out_grad_grouped = mixture_grad.reshape(span_rows, shared_heads, group_size, HD)
    delta = jnp.sum(
        out_grad_grouped.astype(jnp.float32).transpose(1, 2, 0, 3) * out_grouped, axis=-1
    )

    def visit_source(turn_number, state_now):
        key_now, value_now, key_acc, value_acc, query_acc = state_now
        source = (block_index - turn_number) % block_count
        block_start = source * span_rows
        key_block = key_now.reshape(span_rows, shared_heads, HD)
        value_block = value_now.reshape(span_rows, shared_heads, HD)

        def contribute(accums):
            key_acc_in, value_acc_in, query_acc_in = accums
            scores = (
                jnp.einsum(
                    "qkgd,skd->kgqs", query_grouped, key_block, preferred_element_type=jnp.float32
                )
                * score_scale
            )
            allowed = (block_start + key_offsets)[None, :] <= query_place[:, None]
            probability = jnp.where(allowed, jnp.exp(scores - log_total[..., None]), 0.0)
            value_part = jnp.einsum(
                "kgqs,qkgd->skd",
                probability.astype(jnp.bfloat16),
                out_grad_grouped,
                preferred_element_type=jnp.float32,
            )
            prob_grad = jnp.einsum(
                "qkgd,skd->kgqs", out_grad_grouped, value_block, preferred_element_type=jnp.float32
            )
            score_grad = (probability * (prob_grad - delta[..., None])).astype(jnp.bfloat16)
            query_acc_out = (
                query_acc_in
                + jnp.einsum(
                    "kgqs,skd->kgqd", score_grad, key_block, preferred_element_type=jnp.float32
                )
                * score_scale
            )
            key_part = (
                jnp.einsum(
                    "kgqs,qkgd->skd", score_grad, query_grouped, preferred_element_type=jnp.float32
                )
                * score_scale
            )
            return (
                key_acc_in + key_part.reshape(span_rows, -1),
                value_acc_in + value_part.reshape(span_rows, -1),
                query_acc_out,
            )

        key_acc, value_acc, query_acc = lax.cond(
            source <= block_index,
            contribute,
            lambda accums: accums,
            (key_acc, value_acc, query_acc),
        )
        key_now, value_now = from_behind((key_now, value_now), "blk", 1)
        key_acc, value_acc = (
            shifted(key_acc.astype(jnp.bfloat16), "blk", 1).astype(key_acc.dtype),
            shifted(value_acc.astype(jnp.bfloat16), "blk", 1).astype(value_acc.dtype),
        )
        return (key_now, value_now, key_acc, value_acc, query_acc)

    start_turn = (
        key_heads,
        value_low,
        jnp.zeros((span_rows, shared_heads * HD), jnp.float32),
        jnp.zeros((span_rows, shared_heads * HD), jnp.float32),
        jnp.zeros((shared_heads, group_size, span_rows, HD), jnp.float32),
    )
    unused_keys, unused_values, key_acc, value_acc, query_acc = lax.fori_loop(
        0, block_count, visit_source, start_turn
    )
    query_rows_grad = query_acc.transpose(2, 0, 1, 3).reshape(span_rows, -1).astype(jnp.bfloat16)
    key_tok_grad = key_acc.astype(jnp.bfloat16)
    value_tok_grad = value_acc.astype(jnp.bfloat16)
    query_raw_grad, query_gain_grad = query_back(query_rows_grad.astype(jnp.float32))
    key_raw_grad, key_gain_grad = key_back(key_tok_grad.astype(jnp.float32))
    query_raw_low = query_raw_grad.astype(jnp.bfloat16)
    key_raw_low = key_raw_grad.astype(jnp.bfloat16)
    query_grad = jnp.dot(normed_rows.T, query_raw_low, preferred_element_type=jnp.float32)
    key_grad = jnp.dot(normed_rows.T, key_raw_low, preferred_element_type=jnp.float32)
    value_grad = jnp.dot(normed_rows.T, value_tok_grad, preferred_element_type=jnp.float32)
    normed_grad = (
        jnp.dot(query_raw_low, full_query.T, preferred_element_type=jnp.float32)
        + jnp.dot(key_raw_low, full_key.T, preferred_element_type=jnp.float32)
        + jnp.dot(value_tok_grad, full_value.T, preferred_element_type=jnp.float32)
    )
    normed_grad = sum_tokens(normed_grad)
    input_part, attention_gain_grad = normed_back(normed_grad)
    input_gradient = (hidden_grad + input_part).astype(jnp.bfloat16)
    query_gain_sum, key_gain_sum = lax.psum((query_gain_grad, key_gain_grad), ("head", "blk"))

    def regroup(grad):
        return (
            grad.reshape(head_count, block_count, -1, grad.shape[-1])
            .transpose(1, 0, 2, 3)
            .reshape(grad.shape[0], grad.shape[-1])
        )

    (
        query_part,
        key_part,
        value_part,
        gate_part,
        up_part,
        attention_part,
        feed_part,
        mixing_sum,
        down_sum,
    ) = (
        lax.psum_scatter(
            regroup(query_grad).astype(jnp.bfloat16), "blk", scatter_dimension=0, tiled=True
        ).astype(jnp.float32),
        lax.psum_scatter(
            regroup(key_grad).astype(jnp.bfloat16), "blk", scatter_dimension=0, tiled=True
        ).astype(jnp.float32),
        lax.psum_scatter(
            regroup(value_grad).astype(jnp.bfloat16), "blk", scatter_dimension=0, tiled=True
        ).astype(jnp.float32),
        lax.psum_scatter(
            regroup(gate_grad).astype(jnp.bfloat16), "blk", scatter_dimension=0, tiled=True
        ).astype(jnp.float32),
        lax.psum_scatter(
            regroup(up_grad).astype(jnp.bfloat16), "blk", scatter_dimension=0, tiled=True
        ).astype(jnp.float32),
        lax.psum_scatter(
            regroup(attention_gain_grad[:, None]).astype(jnp.bfloat16),
            "blk",
            scatter_dimension=0,
            tiled=True,
        ).astype(jnp.float32),
        lax.psum_scatter(
            regroup(feed_gain_grad[:, None]).astype(jnp.bfloat16),
            "blk",
            scatter_dimension=0,
            tiled=True,
        ).astype(jnp.float32),
        lax.psum_scatter(
            mixing_grad.astype(jnp.bfloat16), "blk", scatter_dimension=0, tiled=True
        ).astype(jnp.float32),
        lax.psum_scatter(
            down_grad.astype(jnp.bfloat16), "blk", scatter_dimension=0, tiled=True
        ).astype(jnp.float32),
    )
    query_sum, key_sum, value_sum, gate_sum, up_sum, attention_tile, feed_tile = (
        lax.all_to_all(
            query_part.astype(jnp.bfloat16), "head", split_axis=0, concat_axis=1, tiled=True
        ).astype(query_part.dtype),
        lax.all_to_all(
            key_part.astype(jnp.bfloat16), "head", split_axis=0, concat_axis=1, tiled=True
        ).astype(key_part.dtype),
        lax.all_to_all(
            value_part.astype(jnp.bfloat16), "head", split_axis=0, concat_axis=1, tiled=True
        ).astype(value_part.dtype),
        lax.all_to_all(
            gate_part.astype(jnp.bfloat16), "head", split_axis=0, concat_axis=1, tiled=True
        ).astype(gate_part.dtype),
        lax.all_to_all(
            up_part.astype(jnp.bfloat16), "head", split_axis=0, concat_axis=1, tiled=True
        ).astype(up_part.dtype),
        lax.all_to_all(
            attention_part.astype(jnp.bfloat16), "head", split_axis=0, concat_axis=1, tiled=True
        ).astype(attention_part.dtype),
        lax.all_to_all(
            feed_part.astype(jnp.bfloat16), "head", split_axis=0, concat_axis=1, tiled=True
        ).astype(feed_part.dtype),
    )
    attention_gain_sum = jnp.sum(attention_tile, axis=1)
    feed_gain_sum = jnp.sum(feed_tile, axis=1)
    return (
        output,
        input_gradient,
        query_sum,
        key_sum,
        value_sum,
        mixing_sum,
        gate_sum,
        up_sum,
        down_sum,
        attention_gain_sum,
        feed_gain_sum,
        query_gain_sum,
        key_gain_sum,
    )


def solution(mesh):
    in_specs = (
        P(("blk", "head"), None),
        P(("head", "blk"), None),
        P(("head", "blk"), None),
        P(("head", "blk"), None),
        P(("head", "blk"), None),
        P(("head", "blk"), None),
        P(("head", "blk"), None),
        P(("head", "blk"), None),
        P(("head", "blk")),
        P(("head", "blk")),
        P(),
        P(),
        P(("blk", "head"), None),
    )
    out_specs = (
        P(("blk", "head"), None),
        P(("blk", "head"), None),
        P(("head", "blk"), None),
        P(("head", "blk"), None),
        P(("head", "blk"), None),
        P(("head", "blk"), None),
        P(("head", "blk"), None),
        P(("head", "blk"), None),
        P(("head", "blk"), None),
        P(("head", "blk")),
        P(("head", "blk")),
        P(),
        P(),
    )
    return jax.shard_map(
        per_device, mesh=mesh, in_specs=in_specs, out_specs=out_specs, check_vma=False
    )
```

profile of v0, /device:TPU:9, one launch (start us, length us, event | category | flops | bytes accessed | tf_op | source)
XLA Modules:
  0.0 1413.8 jit_solution(8018065907502048134)
XLA Ops:
  173.6 70.3 %while.41 = (s32[]{:T(128)}, f32[2,2,1024]{2,1,0:T(2,128)S(1)}, f32[2,2,1024]{2,1,0:T(2,128)S(1)}, f32[2,2,1024,64]{2,3,1,0:T(8,128)S(1)}, s32[8]{0:T(128)S(1)},...) while((s32[]{:T(128)}, f32[2,2,1024]{2,1,0:T(2,128)S(1)}, ...), condition=%wide.region_8.9_spmd.clone.clone, body=%wide.region_3.8_spmd.clone.clone.sunk | while | flops 1121462272 | bytes 57963808 | solution.py:204
  269.6 92.0 %reduce-scatter.18.cloned.1.call-done = bf16[256,1024]{1,0:T(8,128)(2,1)} async-done(((bf16[1024,1024]{1,0:T(8,128)(2,1)}), bf16[256,1024]{1,0:T(8,128)(2,1)}) %reduce-scatter.18.cloned.1.call-update) | async-done | bytes 524304 | tf_op jit(solution)/shard_map/reduce_scatter | solution.py:75
  365.0 29.8 %all-gather.18.cloned.1.call-done = bf16[256,4608]{1,0:T(8,128)(2,1)} async-done(((bf16[32,4608]{1,0:T(8,128)(2,1)}), bf16[256,4608]{1,0:T(8,128)(2,1)}) %all-gather.18.cloned.1.call-update) | async-done | bytes 2359312 | tf_op jit(solution)/shard_map/all_gather | solution.py:122
  404.2 45.0 %all-gather.24.cloned.1.call-done = bf16[1024,1024]{1,0:T(8,128)(2,1)} async-done(((bf16[256,1024]{1,0:T(8,128)(2,1)}), bf16[1024,1024]{1,0:T(8,128)(2,1)}) %all-gather.24.cloned.1.call-update) | async-done | bytes 2097168 | tf_op jit(solution)/shard_map/all_gather | solution.py:71
  449.2 32.7 %all-gather.22.cloned.1.call-done = bf16[1152,1024]{1,0:T(8,128)(2,1)} async-done(((bf16[144,1024]{1,0:T(8,128)(2,1)}), bf16[1152,1024]{1,0:T(8,128)(2,1)}) %all-gather.22.cloned.1.call-update) | async-done | bytes 2359312 | tf_op jit(solution)/shard_map/all_gather | solution.py:124
  495.6 23.4 %all-gather.16.cloned.1.call-done = bf16[1024,1024]{1,0:T(8,128)(2,1)} async-done(((bf16[256,1024]{1,0:T(8,128)(2,1)}), bf16[1024,1024]{1,0:T(8,128)(2,1)}) %all-gather.16.cloned.1.call-update) | async-done | bytes 2097168 | tf_op jit(solution)/shard_map/all_gather | solution.py:71
  536.9 35.3 %reduce-scatter.22.cloned.1.call-done = bf16[256,1024]{1,0:T(8,128)(2,1)} async-done(((bf16[1024,1024]{1,0:T(8,128)(2,1)}), bf16[256,1024]{1,0:T(8,128)(2,1)}) %reduce-scatter.22.cloned.1.call-update) | async-done | bytes 524304 | tf_op jit(solution)/shard_map/reduce_scatter | solution.py:75
  578.1 33.9 %all-gather.26.cloned.1.call-done = bf16[1024,1024]{1,0:T(8,128)(2,1)} async-done(((bf16[256,1024]{1,0:T(8,128)(2,1)}), bf16[1024,1024]{1,0:T(8,128)(2,1)}) %all-gather.26.cloned.1.call-update) | async-done | bytes 2097168 | tf_op jit(solution)/shard_map/all_gather | solution.py:71
  617.2 400.5 %while.40 = (s32[]{:T(128)}, bf16[1024,128]{0,1:T(8,128)(2,1)S(1)}, bf16[1024,128]{0,1:T(8,128)(2,1)}, f32[1024,128]{0,1:T(8,128)}, f32[1024,128]{0,1:T(8,128)S(...) while((s32[]{:T(128)}, bf16[1024,128]{0,1:T(8,128)(2,1)S(1)}, ...), condition=%wide.region_18.19_spmd.clone, body=%wide.region_15.18_spmd.clone.sunk | while | flops 2729052160 | bytes 101659368 | solution.py:315
  619.2 34.4 %conditional.7 = ((f32[1024,128]{0,1:T(8,128)S(1)}, f32[1024,128]{0,1:T(8,128)S(1)}, f32[2,2,1024,64]{2,3,1,0:T(8,128)S(1)})) conditional(s32[]{:T(128)} %convert_element_type.687, (f32[1024,128]{0,1:T(8,128)S(1)}, f32[1024,128]{0,1:T(8,128)S(1)}, f32[2,2,1024,64]{2,3,1,0:T(8,128)S(1)}) %tuple.128, (s32[]{:T(128)}, s32[1024]{0:T(1024)S(1)}, ...), branch_computations={%region_16.16_spmd, %region_17.17_spmd} | conditional | flops 2728265728 | bytes 91168928 | solution.py:295
  670.1 34.4 %conditional.7 = ((f32[1024,128]{0,1:T(8,128)S(1)}, f32[1024,128]{0,1:T(8,128)S(1)}, f32[2,2,1024,64]{2,3,1,0:T(8,128)S(1)})) conditional(s32[]{:T(128)} %convert_element_type.687, (f32[1024,128]{0,1:T(8,128)S(1)}, f32[1024,128]{0,1:T(8,128)S(1)}, f32[2,2,1024,64]{2,3,1,0:T(8,128)S(1)}) %tuple.128, (s32[]{:T(128)}, s32[1024]{0:T(1024)S(1)}, ...), branch_computations={%region_16.16_spmd, %region_17.17_spmd} | conditional | flops 2728265728 | bytes 91168928 | solution.py:295
  721.8 34.4 %conditional.7 = ((f32[1024,128]{0,1:T(8,128)S(1)}, f32[1024,128]{0,1:T(8,128)S(1)}, f32[2,2,1024,64]{2,3,1,0:T(8,128)S(1)})) conditional(s32[]{:T(128)} %convert_element_type.687, (f32[1024,128]{0,1:T(8,128)S(1)}, f32[1024,128]{0,1:T(8,128)S(1)}, f32[2,2,1024,64]{2,3,1,0:T(8,128)S(1)}) %tuple.128, (s32[]{:T(128)}, s32[1024]{0:T(1024)S(1)}, ...), branch_computations={%region_16.16_spmd, %region_17.17_spmd} | conditional | flops 2728265728 | bytes 91168928 | solution.py:295
  773.4 34.4 %conditional.7 = ((f32[1024,128]{0,1:T(8,128)S(1)}, f32[1024,128]{0,1:T(8,128)S(1)}, f32[2,2,1024,64]{2,3,1,0:T(8,128)S(1)})) conditional(s32[]{:T(128)} %convert_element_type.687, (f32[1024,128]{0,1:T(8,128)S(1)}, f32[1024,128]{0,1:T(8,128)S(1)}, f32[2,2,1024,64]{2,3,1,0:T(8,128)S(1)}) %tuple.128, (s32[]{:T(128)}, s32[1024]{0:T(1024)S(1)}, ...), branch_computations={%region_16.16_spmd, %region_17.17_spmd} | conditional | flops 2728265728 | bytes 91168928 | solution.py:295
  825.1 36.9 %collective-permute-start.3 = (bf16[1024,128]{0,1:T(8,128)(2,1)S(1)}, bf16[1024,128]{0,1:T(8,128)(2,1)S(1)}, u32[]{:S(2)}, u32[]{:S(2)}) collective-permute-start(bf16[1024,128]{0,1:T(8,128)(2,1)S(1)} %convert_element_type.690), channel_id=1, source_target_pairs={{0,1},{1,2},{2,3},{3,4},{4,5},{5,6},{6,7},{7,0},{8,9},{9,10},{10,1... | collective-permute-start | bytes 786440 | tf_op jit(solution)/shard_map/while/body/eval_jaxpr/ppermute | solution.py:27
  879.3 33.5 %collective-permute-start.2 = (bf16[1024,128]{0,1:T(8,128)(2,1)S(1)}, bf16[1024,128]{0,1:T(8,128)(2,1)S(1)}, u32[]{:S(2)}, u32[]{:S(2)}) collective-permute-start(bf16[1024,128]{0,1:T(8,128)(2,1)S(1)} %convert_element_type.688), channel_id=1, source_target_pairs={{0,1},{1,2},{2,3},{3,4},{4,5},{5,6},{6,7},{7,0},{8,9},{9,10},{10,1... | collective-permute-start | bytes 786440 | tf_op jit(solution)/shard_map/while/body/eval_jaxpr/ppermute | solution.py:27
  930.1 38.7 %collective-permute-start = (bf16[1024,128]{0,1:T(8,128)(2,1)S(1)}, bf16[1024,128]{0,1:T(8,128)(2,1)S(1)}, u32[]{:S(2)}, u32[]{:S(2)}) collective-permute-start(bf16[1024,128]{0,1:T(8,128)(2,1)S(1)} %copy.257), channel_id=1, source_target_pairs={{0,1},{1,2},{2,3},{3,4},{4,5},{5,6},{6,7},{8,9},{9,10},{10,11},{11... | collective-permute-start | bytes 786440 | tf_op jit(solution)/shard_map/while/body/eval_jaxpr/ppermute | solution.py:21
  986.2 27.8 %collective-permute-start.1 = (bf16[1024,128]{0,1:T(8,128)(2,1)}, bf16[1024,128]{0,1:T(8,128)(2,1)}, u32[]{:S(2)}, u32[]{:S(2)}) collective-permute-start(bf16[1024,128]{0,1:T(8,128)(2,1)} %copy.258), channel_id=1, source_target_pairs={{0,1},{1,2},{2,3},{3,4},{4,5},{5,6},{6,7},{8,9},{9,10},{10,11},{11... | collective-permute-start | bytes 786440 | tf_op jit(solution)/shard_map/while/body/eval_jaxpr/ppermute | solution.py:21
  1097.9 30.9 %reduce-scatter.36.cloned.1.call-done = bf16[128,1152]{1,0:T(8,128)(2,1)} async-done(((bf16[1024,1152]{1,0:T(8,128)(2,1)}), bf16[128,1152]{1,0:T(8,128)(2,1)}) %reduce-scatter.36.cloned.1.call-update) | async-done | bytes 294928 | tf_op jit(solution)/shard_map/reduce_scatter | solution.py:368
  1133.0 33.5 %reduce-scatter.38.cloned.1.call-done = bf16[144,1024]{1,0:T(8,128)(2,1)} async-done(((bf16[1152,1024]{1,0:T(8,128)(2,1)}), bf16[144,1024]{1,0:T(8,128)(2,1)}) %reduce-scatter.38.cloned.1.call-update) | async-done | bytes 294928 | tf_op jit(solution)/shard_map/reduce_scatter | solution.py:386
  1168.3 36.0 %reduce-scatter.34.cloned.1.call-done = bf16[128,1152]{1,0:T(8,128)(2,1)} async-done(((bf16[1024,1152]{1,0:T(8,128)(2,1)}), bf16[128,1152]{1,0:T(8,128)(2,1)}) %reduce-scatter.34.cloned.1.call-update) | async-done | bytes 294928 | tf_op jit(solution)/shard_map/reduce_scatter | solution.py:365
  1239.6 47.1 %all-reduce.6 = (f32[64]{0:T(128)}, f32[64]{0:T(128)}) all-reduce(f32[64]{0:T(128)} %get-tuple-element.789, f32[64]{0:T(128)} %get-tuple-element.793), channel_id=1, replica_groups=mesh['head'=4,'blk'=8] {'head','blk'}, use_global_device_ids=true, to_apply=%region_37.38 | all-reduce | flops 128 | bytes 1024 | tf_op jit(solution)/shard_map/psum | solution.py:336
  1301.2 27.7 %reduce-scatter.32.cloned.1.call-done = bf16[32,1024]{1,0:T(8,128)(2,1)} async-done(((bf16[256,1024]{1,0:T(8,128)(2,1)}), bf16[32,1024]{1,0:T(8,128)(2,1)}) %reduce-scatter.32.cloned.1.call-update) | async-done | bytes 65552 | tf_op jit(solution)/shard_map/reduce_scatter | solution.py:383
  1331.8 28.1 %reduce-scatter.40.cloned.1.call-done = bf16[128,1]{1,0:T(8,128)(2,1)} async-done(((bf16[1024,1]{1,0:T(8,128)(2,1)}), bf16[128,1]{1,0:T(8,128)(2,1)}) %reduce-scatter.40.cloned.1.call-update) | async-done | bytes 272
  1364.8 38.3 %reduce-scatter.20.cloned.1.call-done = bf16[256,1024]{1,0:T(8,128)(2,1)} async-done(((bf16[1024,1024]{1,0:T(8,128)(2,1)}), bf16[256,1024]{1,0:T(8,128)(2,1)}) %reduce-scatter.20.cloned.1.call-update) | async-done | bytes 524304 | tf_op jit(solution)/shard_map/reduce_scatter | solution.py:75
  (607 shorter events, 779.4 us)
Async XLA Ops:
  56.3 92.5 %all-gather.12.cloned.1.call-start = ((), (), s32[]{:S(2)}) async-start(), calls=%async_computation.28 | async-start | bytes 2359296 | tf_op jit(solution)/shard_map/all_gather | solution.py:167
  77.9 76.4 %all-gather.14.cloned.1.call-start = ((), (), s32[]{:S(2)}) async-start(), calls=%async_computation.29 | async-start | bytes 2359296 | tf_op jit(solution)/shard_map/all_gather | solution.py:168
  102.6 158.9 %all-gather.20.cloned.1.call-start = ((), (), s32[]{:S(2)}) async-start(), calls=%async_computation.33 | async-start | bytes 2654208 | tf_op jit(solution)/shard_map/all_gather | solution.py:123
  127.3 234.3 %reduce-scatter.18.cloned.1.call-start = ((), (), s32[]{:S(2)}) async-start(), calls=%async_computation.30 | async-start | bytes 2621440 | tf_op jit(solution)/shard_map/reduce_scatter | solution.py:75
  246.2 148.6 %all-gather.18.cloned.1.call-start = ((), (), s32[]{:S(2)}) async-start(), calls=%async_computation.32 | async-start | bytes 2654208 | tf_op jit(solution)/shard_map/all_gather | solution.py:122
  246.8 202.4 %all-gather.24.cloned.1.call-start = ((), (), s32[]{:S(2)}) async-start(), calls=%async_computation.36 | async-start | bytes 2621440 | tf_op jit(solution)/shard_map/all_gather | solution.py:71
  247.5 234.4 %all-gather.22.cloned.1.call-start = ((), (), s32[]{:S(2)}) async-start(), calls=%async_computation.34 | async-start | bytes 2654208 | tf_op jit(solution)/shard_map/all_gather | solution.py:124
  265.8 133.3 %all-to-all-start.6 = ((bf16[256,4,1152]{0,2,1:T(8,128)(2,1)}), bf16[256,4,1152]{0,2,1:T(8,128)(2,1)S(1)}, u32[]{:S(2)}, u32[]{:S(2)}) async-start(bf16[256,4,1152]{0,2,1:T(8,128)(2,1)} %bitcast.258), calls=%async_computation.7 | async-start | bytes 4718592 | tf_op jit(solution)/shard_map/all_to_all | solution.py:137
  269.6 249.4 %all-gather.16.cloned.1.call-start = ((), (), s32[]{:S(2)}) async-start(), calls=%async_computation.31 | async-start | bytes 2621440 | tf_op jit(solution)/shard_map/all_gather | solution.py:71
  399.1 91.9 %all-to-all-start.5 = ((bf16[256,4,1152]{0,2,1:T(8,128)(2,1)}), bf16[256,4,1152]{0,2,1:T(8,128)(2,1)}, u32[]{:S(2)}, u32[]{:S(2)}) async-start(bf16[256,4,1152]{0,2,1:T(8,128)(2,1)} %bitcast.259), calls=%async_computation.6 | async-start | bytes 4718592 | tf_op jit(solution)/shard_map/all_to_all | solution.py:136
  404.1 168.0 %reduce-scatter.22.cloned.1.call-start = ((), (), s32[]{:S(2)}) async-start(), calls=%async_computation.37 | async-start | bytes 2621440 | tf_op jit(solution)/shard_map/reduce_scatter | solution.py:75
  536.8 75.2 %all-gather.26.cloned.1.call-start = ((), (), s32[]{:S(2)}) async-start(), calls=%async_computation.38 | async-start | bytes 2621440 | tf_op jit(solution)/shard_map/all_gather | solution.py:71
  576.6 488.6 %reduce-scatter.24.cloned.1.call-start = ((), (), s32[]{:S(2)}) async-start(), calls=%async_computation.39 | async-start | bytes 2621440 | tf_op jit(solution)/shard_map/reduce_scatter | solution.py:75
  1027.5 62.7 %reduce-scatter.42.cloned.1.call-start = ((), (), s32[]{:S(2)}) async-start(), calls=%async_computation.48 | async-start | bytes 294912
  1028.9 99.9 %reduce-scatter.36.cloned.1.call-start = ((), (), s32[]{:S(2)}) async-start(), calls=%async_computation.45 | async-start | bytes 2654208 | tf_op jit(solution)/shard_map/reduce_scatter | solution.py:368
  1035.5 131.0 %reduce-scatter.38.cloned.1.call-start = ((), (), s32[]{:S(2)}) async-start(), calls=%async_computation.46 | async-start | bytes 2654208 | tf_op jit(solution)/shard_map/reduce_scatter | solution.py:386
  1042.8 161.6 %reduce-scatter.34.cloned.1.call-start = ((), (), s32[]{:S(2)}) async-start(), calls=%async_computation.44 | async-start | bytes 2654208 | tf_op jit(solution)/shard_map/reduce_scatter | solution.py:365
  1051.0 183.5 %reduce-scatter.30.cloned.1.call-start = ((), (), s32[]{:S(2)}) async-start(), calls=%async_computation.42 | async-start | bytes 294912 | tf_op jit(solution)/shard_map/reduce_scatter | solution.py:362
  1054.1 232.6 %reduce-scatter.28.cloned.1.call-start = ((), (), s32[]{:S(2)}) async-start(), calls=%async_computation.41 | async-start | bytes 294912 | tf_op jit(solution)/shard_map/reduce_scatter | solution.py:359
  1059.9 237.4 %reduce-scatter.26.cloned.1.call-start = ((), (), s32[]{:S(2)}) async-start(), calls=%async_computation.40 | async-start | bytes 589824 | tf_op jit(solution)/shard_map/reduce_scatter | solution.py:356
  1061.6 267.3 %reduce-scatter.32.cloned.1.call-start = ((), (), s32[]{:S(2)}) async-start(), calls=%async_computation.43 | async-start | bytes 589824 | tf_op jit(solution)/shard_map/reduce_scatter | solution.py:383
  1064.9 295.0 %reduce-scatter.40.cloned.1.call-start = ((), (), s32[]{:S(2)}) async-start(), calls=%async_computation.47 | async-start | bytes 294912
  1068.7 334.4 %reduce-scatter.20.cloned.1.call-start = ((), (), s32[]{:S(2)}) async-start(), calls=%async_computation.35 | async-start | bytes 2621440 | tf_op jit(solution)/shard_map/reduce_scatter | solution.py:75
  1128.8 75.5 %all-to-all-start.11 = ((bf16[4,32,1152]{2,1,0:T(8,128)(2,1)}), bf16[4,32,1152]{2,1,0:T(8,128)(2,1)S(1)}, u32[]{:S(2)}, u32[]{:S(2)}) async-start(bf16[4,32,1152]{2,1,0:T(8,128)(2,1)} %bitcast.296), calls=%async_computation.21 | async-start | bytes 589824 | tf_op jit(solution)/shard_map/all_to_all | solution.py:403
  (129 other events, 3977.8 us)
Sparse Core Ops, SparseCore 0:
  32.4 41.0 all-gather.9
  78.0 30.0 all-gather.11
  109.7 30.7 all-gather.13
  142.0 31.3 all-gather.19
  246.3 115.2 reduce-scatter.17
  363.2 31.5 all-gather.17
  396.8 52.3 all-gather.23
  450.9 30.9 all-gather.21
  484.5 34.4 all-gather.15
  536.9 35.1 reduce-scatter.21
  576.7 35.2 all-gather.25
  1027.6 35.8 reduce-scatter.23
  1066.5 23.7 reduce-scatter.41
  1092.4 36.3 reduce-scatter.35
  1131.0 35.4 reduce-scatter.37
  1168.7 35.6 reduce-scatter.33
  1207.0 27.4 reduce-scatter.29
  1236.7 28.5 reduce-scatter.27
  1268.1 29.1 reduce-scatter.25
  1300.1 28.8 reduce-scatter.31
  1331.2 28.6 reduce-scatter.39
  1363.1 39.9 reduce-scatter.19
where the time goes:
time: 1430 us; the launch traced here: 1410 us
  waiting for transfers between devices  592 us (41%)
  starting transfers between devices  237 us (17%)
  matrix products  237 us (17%)
  blocking collectives  154 us (11%)
  local copies, waits for them, and re-layouts  92 us (6%)
  other arithmetic  77.5 us (5%)
  between operations  16.6 us (1%)
    reduce_scatter x4, waiting for transfers between devices, sum_tokens(): lax.psum_scatter(values.astype(jnp.bfloat16), 'head', scatter_dimension=0...  166 us
    all_gather x4, waiting for transfers between devices, gather_tokens(): return lax.all_gather(values, 'head', axis=0, tiled=True)  113 us
    ppermute x16, starting transfers between devices, from_behind(): return lax.ppermute(shard, axis, pairs)  106 us
    ppermute x16, starting transfers between devices, shifted(): return lax.ppermute(value, axis, pairs)  90.2 us
    psum x1, blocking collectives, per_device(): lax.psum((query_gain_grad, key_gain_grad), ('head', 'blk'))  47.1 us
    unnamed x24, waiting for transfers between devices  45.7 us
    dot_general x4, matrix products, contribute(): jnp.einsum('kgqs,qkgd->skd', probability.astype(jnp.bfloat16), out_grad_g...  42 us
    dot_general x4, matrix products, contribute(): jnp.einsum('qkgd,skd->kgqs', out_grad_grouped, value_block, preferred_ele...  37.1 us
  transfers between devices with their start and end apart: 65, of which 41 were waited for; matrix products, arithmetic and copies ran while one was open for 14% of the time, Pallas kernels for 0%

commit v1 on v0

v1 whole, which is shorter than its diff:
```python
import functools
import math

import jax
import jax.numpy as jnp
from jax import lax
from jax.experimental import pallas as pl
from jax.experimental.pallas import tpu as pltpu
from jax.sharding import PartitionSpec as P

HQ = 16
KV = 8
HD = 64
EPSILON = 1e-05
ROPE_BASE = 1000000.0
TILE = 1024
QUERY_UNIT = math.log2(math.e) * HD**-0.5

BF = jnp.bfloat16
F32 = jnp.float32
NT = (((1,), (1,)), ((), ()))
NN = (((1,), (0,)), ((), ()))
TN = (((0,), (0,)), ((), ()))
VM = pl.BlockSpec(memory_space=pltpu.VMEM)
SM = pl.BlockSpec(memory_space=pltpu.SMEM)


def dot(a, b, dims=NN):
    return lax.dot_general(a, b, dims, preferred_element_type=F32)


def attend_body(span, local, off_ref, q_ref, kv_ref, acc_ref, out_ref, ones_ref):
    lane = lax.broadcasted_iota(jnp.int32, ones_ref.shape, 1)
    ones_ref[...] = jnp.where(lane < HD, jnp.ones((), BF), kv_ref[...])
    out_ref[...] = jnp.zeros_like(out_ref) if local else acc_ref[...]

    heads = q_ref.shape[0]
    block = min(span, TILE)

    def block_pair(head, q_off, k_off):
        rows = pl.ds(q_off, block)
        keys = pl.ds(k_off, block)
        weight = jnp.exp2(dot(q_ref[head, rows, :], kv_ref[keys, :], NT)).astype(BF)
        out_ref[head, rows, :] += dot(weight, ones_ref[keys, :])

    def full(q_off, k_off):
        for i in range(span // block):
            for j in range(span // block):

                def body(head, carry):
                    block_pair(head, q_off + i * block, k_off + j * block)
                    return carry

                lax.fori_loop(0, heads, body, 0)

    def diagonal(start):
        for i in range(span // block):
            for j in range(i):
                for head in range(heads):
                    block_pair(head, start + i * block, start + j * block)
            diagonal_block(start + i * block)

    def diagonal_block(start):
        size = 256
        for head in range(heads):
            for i in range(block // size):
                rows = slice(start + i * size, start + (i + 1) * size)
                total = None
                pieces = ([(0, i * size)] if i else []) + [(i * size, (i + 1) * size)]
                for low, high in pieces:
                    keys = slice(start + low, start + high)
                    weight = jnp.exp2(dot(q_ref[head, rows, :], kv_ref[keys, :], NT))
                    if low == i * size:
                        place = lax.broadcasted_iota(jnp.int32, (size, size), 0)
                        other = lax.broadcasted_iota(jnp.int32, (size, size), 1)
                        weight = jnp.where(other <= place, weight, 0.0)
                    part = dot(weight.astype(BF), ones_ref[keys, :])
                    total = part if total is None else total + part
                out_ref[head, rows, :] += total

    if local:
        diagonal(0)
        diagonal(span)
        full(pl.multiple_of(off_ref[0], span), pl.multiple_of(off_ref[1], span))
    else:
        for pair in range(2):
            full(
                pl.multiple_of(off_ref[2 * pair], span), pl.multiple_of(off_ref[2 * pair + 1], span)
            )


def attend(offsets, query, kv, acc):
    span = query.shape[1] // 2
    local = acc is None
    if local:

        def body(off_ref, q_ref, kv_ref, out_ref, ones_ref):
            attend_body(span, True, off_ref, q_ref, kv_ref, None, out_ref, ones_ref)
    else:
        body = functools.partial(attend_body, span, False)
    args = (offsets, query, kv) if local else (offsets, query, kv, acc)
    return pl.pallas_call(
        body,
        out_shape=jax.ShapeDtypeStruct(query.shape, F32),
        in_specs=[SM] + [VM] * (len(args) - 1),
        out_specs=VM,
        scratch_shapes=[pltpu.VMEM((2 * span, 2 * HD), BF)],
        cost_estimate=pl.CostEstimate(
            flops=2 * 2 * 2 * 2 * span * span * 256,
            bytes_accessed=8 << 20,
            transcendentals=4 * span * span,
        ),
        compiler_params=pltpu.CompilerParams(vmem_limit_bytes=40 << 20),
    )(*args)


def attend_back_body(
    span, local, off_ref, q_ref, do_ref, kv_ref, acc_ref, dq_ref, dkv_ref, ones_ref, dv_ref
):
    lane = lax.broadcasted_iota(jnp.int32, ones_ref.shape, 1)
    zero = jnp.zeros((), BF)
    ones_ref[...] = jnp.where(
        lane < HD, jnp.where(lane < 3, jnp.ones((), BF), zero), kv_ref[...]
    )
    heads = q_ref.shape[0]
    block = min(span, TILE)
    for head in range(heads):
        dv_ref[head] = jnp.where(lane < HD, zero, do_ref[head])
    dq_ref[...] = jnp.zeros_like(dq_ref) if local else acc_ref[...]
    dkv_ref[...] = jnp.zeros_like(dkv_ref)

    def tile(head, rows, keys, mask):
        query = q_ref[head, rows, :]
        pair = kv_ref[keys, :]
        weight = jnp.exp2(dot(pair, query, NT))
        if mask is not None:
            weight = jnp.where(mask, weight, 0.0)
        score_grad = (weight * dot(ones_ref[keys, :], do_ref[head, rows, :], NT)).astype(BF)
        dkv_ref[keys, :] += dot(weight.astype(BF), dv_ref[head, rows, :]) + dot(score_grad, query)
        dq_ref[head, rows, :] += dot(score_grad, pair, TN)

    def block_pair(head, q_off, k_off):
        tile(head, pl.ds(q_off, block), pl.ds(k_off, block), None)

    def full(q_off, k_off):
        for i in range(span // block):
            for j in range(span // block):

                def body(head, carry):
                    block_pair(head, q_off + i * block, k_off + j * block)
                    return carry

                lax.fori_loop(0, heads, body, 0)

    def diagonal(start):
        for i in range(span // block):
            for j in range(i):
                for head in range(heads):
                    block_pair(head, start + i * block, start + j * block)
            diagonal_block(start + i * block)

    def diagonal_block(start):
        size = 256
        for head in range(heads):
            for i in range(block // size):
                rows = slice(start + i * size, start + (i + 1) * size)
                pieces = ([(0, i * size)] if i else []) + [(i * size, (i + 1) * size)]
                for low, high in pieces:
                    mask = None
                    if low == i * size:
                        key_place = lax.broadcasted_iota(jnp.int32, (size, size), 0)
                        mask = key_place <= lax.broadcasted_iota(jnp.int32, (size, size), 1)
                    tile(head, rows, slice(start + low, start + high), mask)

    if local:
        diagonal(0)
        diagonal(span)
        full(pl.multiple_of(off_ref[0], span), pl.multiple_of(off_ref[1], span))
    else:
        for pair in range(2):
            full(
                pl.multiple_of(off_ref[2 * pair], span), pl.multiple_of(off_ref[2 * pair + 1], span)
            )


def attend_back(offsets, query, out_grad, kv, acc):
    span = query.shape[1] // 2
    local = acc is None
    if local:

        def body(off_ref, q_ref, do_ref, kv_ref, *rest):
            attend_back_body(span, True, off_ref, q_ref, do_ref, kv_ref, None, *rest)
    else:
        body = functools.partial(attend_back_body, span, False)
    args = (offsets, query, out_grad, kv) if local else (offsets, query, out_grad, kv, acc)
    return pl.pallas_call(
        body,
        out_shape=(
            jax.ShapeDtypeStruct(query.shape, F32),
            jax.ShapeDtypeStruct(kv.shape, F32),
        ),
        in_specs=[SM] + [VM] * (len(args) - 1),
        out_specs=(VM, VM),
        scratch_shapes=[
            pltpu.VMEM((2 * span, 2 * HD), BF),
            pltpu.VMEM(query.shape, BF),
        ],
        cost_estimate=pl.CostEstimate(
            flops=5 * 2 * 2 * 2 * span * span * 256,
            bytes_accessed=8 << 20,
            transcendentals=4 * span * span,
        ),
        compiler_params=pltpu.CompilerParams(vmem_limit_bytes=48 << 20),
    )(*args)


def swap_halves(x):
    lane = lax.broadcasted_iota(jnp.int32, x.shape, 1)
    return jnp.where(
        lane % HD < HD // 2, pltpu.roll(x, x.shape[1] - HD // 2, 1), pltpu.roll(x, HD // 2, 1)
    )


def head_mean(x):
    lane = lax.broadcasted_iota(jnp.int32, x.shape, 1)
    low = lane < HD
    first = jnp.sum(jnp.where(low, x, 0.0), axis=1, keepdims=True)
    second = jnp.sum(jnp.where(low, 0.0, x), axis=1, keepdims=True)
    return jnp.where(low, first, second) * (1.0 / HD)


def project_body(x_ref, gain_ref, w_ref, cos_ref, sin_ref, head_gain_ref, normed_ref, raw_ref, pk_ref):
    x = x_ref[...].astype(F32)
    scale = lax.rsqrt(jnp.mean(x * x, axis=1, keepdims=True) + EPSILON)
    normed = (x * scale * gain_ref[...]).astype(BF)
    normed_ref[...] = normed
    raw = dot(normed, w_ref[...])
    raw_ref[...] = raw
    cosine, sine = cos_ref[...], sin_ref[...]
    lane = lax.broadcasted_iota(jnp.int32, cosine.shape, 1)
    for j in range(2):
        query = raw[:, 256 * j : 256 * j + 128]
        pair = raw[:, 256 * j + 128 : 256 * j + 256]
        query = query * lax.rsqrt(head_mean(query * query) + EPSILON) * head_gain_ref[0:1, :]
        query = query * cosine + swap_halves(query) * sine
        pk_ref[j, :, 0:128] = (query * QUERY_UNIT).astype(BF)
        key = pair * lax.rsqrt(head_mean(pair * pair) + EPSILON) * head_gain_ref[1:2, :]
        key = key * cosine + swap_halves(key) * sine
        pk_ref[j, :, 128:256] = jnp.where(lane < HD, key, pair).astype(BF)


def project(x, gain, weight, cosine, sine, head_gain):
    rows, depth = x.shape
    cols = weight.shape[1]
    tile = 256
    return pl.pallas_call(
        project_body,
        grid=(rows // tile,),
        in_specs=[
            pl.BlockSpec((tile, depth), lambda i: (i, 0)),
            pl.BlockSpec((1, depth), lambda i: (0, 0)),
            pl.BlockSpec((depth, cols), lambda i: (0, 0)),
            pl.BlockSpec((tile, 128), lambda i: (i, 0)),
            pl.BlockSpec((tile, 128), lambda i: (i, 0)),
            pl.BlockSpec((8, 128), lambda i: (0, 0)),
        ],
        out_specs=(
            pl.BlockSpec((tile, depth), lambda i: (i, 0)),
            pl.BlockSpec((tile, cols), lambda i: (i, 0)),
            pl.BlockSpec((2, tile, 256), lambda i: (0, i, 0)),
        ),
        out_shape=(
            jax.ShapeDtypeStruct((rows, depth), BF),
            jax.ShapeDtypeStruct((rows, cols), F32),
            jax.ShapeDtypeStruct((2, rows, 256), BF),
        ),
        cost_estimate=pl.CostEstimate(
            flops=4 * rows * depth * cols, bytes_accessed=8 << 20, transcendentals=0
        ),
        compiler_params=pltpu.CompilerParams(vmem_limit_bytes=32 << 20),
    )(x, gain, weight, cosine, sine, head_gain)


def project_back_body(
    raw_ref, grad_ref, normed_ref, w_ref, cos_ref, sin_ref, head_gain_ref,
    part_ref, dw_ref, gain_grad_ref, acc_ref
):
    step = pl.program_id(0)

    @pl.when(step == 0)
    def start():
        acc_ref[...] = jnp.zeros_like(acc_ref)
        gain_grad_ref[...] = jnp.zeros_like(gain_grad_ref)

    cosine, sine = cos_ref[...], sin_ref[...]
    lane = lax.broadcasted_iota(jnp.int32, cosine.shape, 1)
    pieces = []
    gain_sums = [jnp.zeros((1, 128), F32), jnp.zeros((1, 128), F32)]
    for j in range(2):
        for kind in range(2):
            cols = slice(256 * j + 128 * kind, 256 * j + 128 * kind + 128)
            raw = raw_ref[:, cols]
            upstream = grad_ref[j, :, 128 * kind : 128 * kind + 128]
            turned = upstream.astype(F32)
            turned = turned * cosine - swap_halves(turned) * sine
            scale = lax.rsqrt(head_mean(raw * raw) + EPSILON)
            unit = raw * scale
            gain_sums[kind] += jnp.sum(turned * unit, axis=0, keepdims=True)
            turned = turned * head_gain_ref[kind : kind + 1, :]
            grad = scale * (turned - unit * head_mean(turned * unit))
            grad = grad.astype(BF)
            if kind == 1:
                grad = jnp.where(lane < HD, grad, upstream)
            pieces.append(grad)
    gain_grad_ref[0:1, :] += gain_sums[0]
    gain_grad_ref[1:2, :] += gain_sums[1]
    grads = jnp.concatenate(pieces, axis=1)
    part_ref[...] = dot(grads, w_ref[...], NT).astype(BF)
    acc_ref[...] += dot(normed_ref[...], grads, TN)

    @pl.when(step == pl.num_programs(0) - 1)
    def finish():
        dw_ref[...] = acc_ref[...].astype(BF)


def project_back(raw, grad, normed, weight, cosine, sine, head_gain):
    rows, depth = normed.shape
    cols = weight.shape[1]
    tile = 256
    return pl.pallas_call(
        project_back_body,
        grid=(rows // tile,),
        in_specs=[
            pl.BlockSpec((tile, cols), lambda i: (i, 0)),
            pl.BlockSpec((2, tile, 256), lambda i: (0, i, 0)),
            pl.BlockSpec((tile, depth), lambda i: (i, 0)),
            pl.BlockSpec((depth, cols), lambda i: (0, 0)),
            pl.BlockSpec((tile, 128), lambda i: (i, 0)),
            pl.BlockSpec((tile, 128), lambda i: (i, 0)),
            pl.BlockSpec((8, 128), lambda i: (0, 0)),
        ],
        out_specs=(
            pl.BlockSpec((tile, depth), lambda i: (i, 0)),
            pl.BlockSpec((depth, cols), lambda i: (0, 0)),
            pl.BlockSpec((8, 128), lambda i: (0, 0)),
        ),
        out_shape=(
            jax.ShapeDtypeStruct((rows, depth), BF),
            jax.ShapeDtypeStruct((depth, cols), BF),
            jax.ShapeDtypeStruct((8, 128), F32),
        ),
        scratch_shapes=[pltpu.VMEM((depth, cols), F32)],
        cost_estimate=pl.CostEstimate(
            flops=8 * rows * depth * cols, bytes_accessed=8 << 20, transcendentals=0
        ),
        compiler_params=pltpu.CompilerParams(vmem_limit_bytes=40 << 20),
    )(raw, grad, normed, weight, cosine, sine, head_gain)


def permute(x, axis, move):
    count = lax.axis_size(axis)
    return lax.ppermute(x, axis, [(i, move(i) % count) for i in range(count)])


def gather_head(x, place):
    if lax.axis_size("head") != 4:
        return lax.all_gather(x, "head", axis=0, tiled=True)
    half = x.shape[0] // 2
    one = permute(x, "head", lambda i: i ^ 1)
    two = permute(x, "head", lambda i: i ^ 2)
    upper = permute(one[:half], "head", lambda i: i ^ 2)
    lower = permute(two[half:], "head", lambda i: i ^ 1)
    rows = x.shape[0]
    out = jnp.zeros((4 * rows, x.shape[1]), x.dtype)
    for part, other, shift in ((x, 0, 0), (one, 1, 0), (two, 2, 0), (upper, 3, 0), (lower, 3, half)):
        out = lax.dynamic_update_slice(out, part, ((place ^ other) * rows + shift, 0))
    return out


def sum_head(x, place):
    if lax.axis_size("head") != 4:
        return lax.psum_scatter(x, "head", scatter_dimension=0, tiled=True).astype(F32)
    rows = x.shape[0] // 4
    half = rows // 2

    def piece(other, shift):
        return lax.dynamic_slice(x, ((place ^ other) * rows + shift, 0), (half, x.shape[1]))

    first = permute(
        jnp.concatenate([piece(1, 0), piece(3, 0)], axis=0), "head", lambda i: i ^ 1
    ).astype(F32)
    second = permute(
        jnp.concatenate([piece(2, half), piece(3, half)], axis=0), "head", lambda i: i ^ 2
    ).astype(F32)
    upper_far = (first[half:] + piece(2, 0).astype(F32)).astype(BF)
    lower_far = (second[half:] + piece(1, half).astype(F32)).astype(BF)
    upper = permute(upper_far, "head", lambda i: i ^ 2).astype(F32)
    lower = permute(lower_far, "head", lambda i: i ^ 1).astype(F32)
    return jnp.concatenate(
        [
            piece(0, 0).astype(F32) + first[:half] + upper,
            piece(0, half).astype(F32) + second[:half] + lower,
        ],
        axis=0,
    )


def mirror(x):
    count = lax.axis_size("blk")
    return permute(x, "blk", lambda i: count - i if i % 2 else i)


def per_device(
    inputs,
    query_weight,
    key_weight,
    value_weight,
    mixing_weight,
    gate_weight,
    up_weight,
    down_weight,
    attention_gain,
    feedforward_gain,
    query_gain,
    key_gain,
    cotangent,
):
    heads = lax.axis_size("head")
    blocks = lax.axis_size("blk")
    chips = blocks // 2
    place = lax.axis_index("head")
    block = lax.axis_index("blk")
    core = block % 2
    chip = block // 2
    rows, depth = inputs.shape
    span = rows * heads
    piece = query_weight.shape[0]
    width = gate_weight.shape[1] // heads
    shared = KV // heads
    unit_heads = HQ // heads // 2
    unit_cols = unit_heads * HD

    def other_core(x):
        return permute(x, "blk", lambda i: i ^ 1)

    def by_core(mine, theirs):
        first = core == 0
        return jnp.stack([jnp.where(first, mine, theirs), jnp.where(first, theirs, mine)])

    low_rows = lax.all_gather(jnp.concatenate([mixing_weight, down_weight], axis=0), "blk", axis=0)
    mixing_rows = low_rows[:, :piece].reshape(blocks * piece, depth)
    down_full = low_rows[:, piece:].reshape(-1, depth)

    qkv_own = jnp.concatenate(
        [
            jnp.pad(
                query_weight.reshape(piece, heads, 2, unit_cols),
                ((0, 0), (0, 0), (0, 0), (0, 128 - unit_cols)),
            ),
            jnp.repeat(key_weight.reshape(piece, heads, shared, HD), 2 // shared, axis=2),
            jnp.repeat(value_weight.reshape(piece, heads, shared, HD), 2 // shared, axis=2),
        ],
        axis=-1,
    ).reshape(piece, heads, 512)
    gains = jnp.pad(jnp.stack([attention_gain, feedforward_gain], axis=1), ((0, 0), (0, 126)))
    qkv_send = jnp.concatenate(
        [qkv_own, jnp.broadcast_to(gains[:, None, :], (piece, heads, 128))], axis=-1
    ).transpose(1, 0, 2)
    qkv_piece = lax.all_to_all(qkv_send, "head", 0, 0, tiled=True)
    gate_up_send = jnp.concatenate(
        [gate_weight.reshape(piece, heads, width), up_weight.reshape(piece, heads, width)], axis=-1
    ).transpose(1, 0, 2)
    gate_up_piece = lax.all_to_all(gate_up_send, "head", 0, 0, tiled=True)
    qkv_ext = lax.all_gather(qkv_piece, "blk", axis=1).reshape(depth, 640)
    qkv_full = qkv_ext[:, :512]
    attention_row = qkv_ext[:, 512].astype(F32)[None, :]
    feed_row = qkv_ext[:, 513].astype(F32)[None, :]
    gate_up = lax.all_gather(gate_up_piece, "blk", axis=1).reshape(depth, 2 * width)

    span_index = jnp.where(core == 0, block, blocks - block)
    positions = (span_index * span + jnp.arange(span, dtype=jnp.int32)).astype(F32)
    lane = jnp.arange(128, dtype=jnp.int32)
    frequency = jnp.exp(
        (lane % (HD // 2)).astype(F32) * (-2.0 * math.log(ROPE_BASE) / HD)
    )
    angles = positions[:, None] * frequency[None, :]
    cosine = jnp.cos(angles)
    sine = jnp.sin(angles) * jnp.where(lane % HD < HD // 2, -1.0, 1.0)
    head_gain = jnp.concatenate(
        [
            jnp.tile(query_gain.astype(F32), 2)[None, :],
            jnp.tile(key_gain.astype(F32), 2)[None, :],
            jnp.zeros((6, 128), F32),
        ],
        axis=0,
    )

    own = mirror(inputs)
    own_float = own.astype(F32)
    gathered = gather_head(own, place)
    normed, raw, packet = project(gathered, attention_row, qkv_full, cosine, sine, head_gain)

    def to_pairs(x):
        keep = jnp.where(core == 0, x[0], x[1])
        send = jnp.where(core == 0, x[1], x[0])
        return by_core(keep, other_core(send))

    both = to_pairs(packet).reshape(2 * span, 256)
    kv = both[:, 128:]
    zeros = jnp.zeros((2 * span, HD), BF)
    query = jnp.stack(
        [
            jnp.concatenate([both[:, HD * i : HD * (i + 1)], zeros], axis=1)
            for i in range(unit_heads)
        ]
    )

    def low_slot(z):
        return (4 * z >= blocks).astype(jnp.int32)

    def reach(z):
        return jnp.abs(4 * z - (blocks - 1))

    my_low = low_slot(chip)
    my_high = 1 - my_low

    def offsets(step):
        if step == 0:
            return span * jnp.stack([my_high, my_low])
        source = (chip - step) % chips
        low = low_slot(source)
        outer = reach(source) > reach(chip)
        return span * jnp.stack(
            [
                jnp.where(outer, my_low, my_high),
                low,
                my_high,
                jnp.where(outer, low, 1 - low),
            ]
        )

    def next_chip(x):
        return permute(x, "blk", lambda i: i + 2)

    kv_parts = [kv]
    for step in range(1, chips):
        kv_parts.append(next_chip(kv_parts[-1]))
    acc = None
    for step in range(chips):
        acc = attend(offsets(step), query, kv_parts[step], acc)
    total = acc[:, :, 0:1]
    mixture_float = acc[:, :, HD:] / total
    mixture_heads = mixture_float.astype(BF)
    mixture_rows = jnp.concatenate(list(mixture_heads), axis=1).reshape(2, span, unit_cols)

    def from_pairs(x):
        keep = jnp.where(core == 0, x[0], x[1])
        send = jnp.where(core == 0, x[1], x[0])
        return by_core(keep, other_core(send))

    mixture_two = from_pairs(mixture_rows)
    mixture_span = jnp.concatenate([mixture_two[0], mixture_two[1]], axis=1)
    mixture = lax.all_to_all(mixture_span, "head", 0, 1, tiled=True)
    mixing_full = gather_head(mixing_rows, place)
    hidden = own_float + dot(mixture, mixing_full)
    hidden_scale = lax.rsqrt(jnp.mean(hidden * hidden, axis=1, keepdims=True) + EPSILON)
    normed_ffn = (hidden * hidden_scale * feed_row).astype(BF)
    ffn_rows = gather_head(normed_ffn, place)
    own_cot = mirror(cotangent)
    cot_rows = gather_head(own_cot, place)
    gate_value = dot(ffn_rows, gate_up[:, :width])
    up_value = dot(ffn_rows, gate_up[:, width:])
    gate_sigmoid = jax.nn.sigmoid(gate_value)
    activation = (gate_value * gate_sigmoid * up_value).astype(BF)
    activation_grad = dot(cot_rows, down_full, NT).astype(BF).astype(F32)
    gate_grad = (
        activation_grad * up_value * gate_sigmoid * (1.0 + gate_value * (1.0 - gate_sigmoid))
    ).astype(BF)
    up_grad = (activation_grad * gate_value * gate_sigmoid).astype(BF)
    gate_up_grad = jnp.concatenate([gate_grad, up_grad], axis=1)
    normed_ffn_grad = sum_head(dot(gate_up_grad, gate_up, NT).astype(BF), place)

    down_term = sum_head(dot(activation, down_full).astype(BF), place)
    output = mirror((hidden + down_term).astype(BF))
    down_grad = dot(activation, cot_rows, TN).astype(BF)
    down_sum = lax.psum_scatter(down_grad, "blk", scatter_dimension=0, tiled=True).astype(F32)

    def regroup(grad):
        return (
            grad.reshape(heads, blocks, piece, grad.shape[-1])
            .transpose(1, 0, 2, 3)
            .reshape(grad.shape)
        )

    def to_owner(grad):
        part = lax.psum_scatter(regroup(grad), "blk", scatter_dimension=0, tiled=True)
        part = lax.all_to_all(
            part.reshape(heads, piece, -1), "head", split_axis=0, concat_axis=0, tiled=True
        )
        return part.astype(F32)

    gate_up_sum = to_owner(dot(ffn_rows, gate_up_grad, TN).astype(BF))

    unit_ffn = hidden * hidden_scale
    lifted = normed_ffn_grad * feed_row
    hidden_grad = own_cot.astype(F32) + hidden_scale * (
        lifted - unit_ffn * jnp.mean(lifted * unit_ffn, axis=1, keepdims=True)
    )
    hidden_low = hidden_grad.astype(BF)
    mixture_grad = dot(hidden_low, mixing_full, NT).astype(BF)
    hidden_rows = gather_head(hidden_low, place)
    mixing_grad = dot(mixture_span, hidden_rows, TN).astype(BF)
    mixing_sum = lax.psum_scatter(mixing_grad, "blk", scatter_dimension=0, tiled=True).astype(F32)

    grad_span = lax.all_to_all(mixture_grad, "head", 1, 0, tiled=True)
    grad_rows = to_pairs(
        jnp.stack([grad_span[:, :unit_cols], grad_span[:, unit_cols:]])
    ).reshape(2 * span, unit_cols)
    grad_heads = jnp.stack(
        [grad_rows[:, HD * i : HD * (i + 1)] for i in range(unit_heads)]
    ).astype(F32)
    inverse = 1.0 / total
    shift = jnp.sum(grad_heads * mixture_float, axis=-1, keepdims=True) * (-inverse)
    shift_high = shift.astype(BF)
    rest = shift - shift_high.astype(F32)
    shift_mid = rest.astype(BF)
    shift_low = (rest - shift_mid.astype(F32)).astype(BF)
    out_grad = jnp.concatenate(
        [
            shift_high,
            shift_mid,
            shift_low,
            jnp.zeros((unit_heads, 2 * span, HD - 3), BF),
            (grad_heads * inverse).astype(BF),
        ],
        axis=-1,
    )
    query_acc = None
    travelling = None
    for step in list(range(1, chips)) + [0]:
        args = (offsets(step), query, out_grad, kv_parts[step])
        if query_acc is None:
            query_acc, kv_grad = attend_back(
                *args, jnp.zeros(query.shape, F32) if step else None
            )
        else:
            if step == 0:
                local_acc, kv_grad = attend_back(*args, None)
                query_acc = query_acc + local_acc
            else:
                query_acc, kv_grad = attend_back(*args, query_acc)
        if travelling is not None:
            kv_grad = kv_grad + travelling.astype(F32)
        if step:
            travelling = next_chip(kv_grad.astype(BF))
    query_rows_grad = jnp.concatenate(
        [query_acc[i, :, :HD] for i in range(unit_heads)]
        + [jnp.zeros((2 * span, 128 - unit_cols), F32)],
        axis=1,
    ) * (HD**-0.5)
    key_unit = jnp.where(lane < HD, math.log(2.0), 1.0)[None, :]
    grads = jnp.concatenate(
        [query_rows_grad.astype(BF), (kv_grad * key_unit).astype(BF)], axis=1
    ).reshape(2, span, 256)
    grads = from_pairs(grads)
    normed_part, qkv_grad, head_gain_grad = project_back(
        raw, grads, normed, qkv_full, cosine, sine, head_gain
    )
    normed_grad = sum_head(normed_part, place)
    input_scale = lax.rsqrt(jnp.mean(own_float * own_float, axis=1, keepdims=True) + EPSILON)
    unit = own_float * input_scale
    lifted = normed_grad * attention_row
    input_gradient = hidden_grad + input_scale * (
        lifted - unit * jnp.mean(lifted * unit, axis=1, keepdims=True)
    )
    input_gradient = mirror(input_gradient.astype(BF))

    head_gain_grad = head_gain_grad[:2, :]
    bit = 1
    while bit < heads:
        head_gain_grad += permute(head_gain_grad, "head", lambda i, bit=bit: i ^ bit)
        bit *= 2
    bit = 1
    while bit < blocks:
        head_gain_grad += permute(head_gain_grad, "blk", lambda i, bit=bit: i ^ bit)
        bit *= 2
    query_gain_sum = head_gain_grad[0, :HD] + head_gain_grad[0, HD:]
    key_gain_sum = head_gain_grad[1, :HD]

    qkv_sum = to_owner(qkv_grad)
    attention_gain_sum = jnp.sum(
        qkv_sum * qkv_own.transpose(1, 0, 2).astype(F32), axis=(0, 2)
    ) / attention_gain.astype(F32)
    feed_gain_sum = jnp.sum(
        gate_up_sum * gate_up_send.astype(F32), axis=(0, 2)
    ) / feedforward_gain.astype(F32)
    qkv_cols = qkv_sum.transpose(1, 0, 2).reshape(piece, heads, 2, 256)
    gate_up_cols = gate_up_sum.transpose(1, 0, 2)

    def per_head(cols):
        return cols.reshape(piece, heads, shared, 2 // shared, HD).sum(axis=3).reshape(piece, -1)

    return (
        output,
        input_gradient,
        qkv_cols[..., :unit_cols].reshape(piece, -1),
        per_head(qkv_cols[..., 128 : 128 + HD]),
        per_head(qkv_cols[..., 128 + HD :]),
        mixing_sum,
        gate_up_cols[..., :width].reshape(piece, -1),
        gate_up_cols[..., width:].reshape(piece, -1),
        down_sum,
        attention_gain_sum,
        feed_gain_sum,
        query_gain_sum,
        key_gain_sum,
    )


def solution(mesh):
    in_specs = (
        P(("blk", "head"), None),
        P(("head", "blk"), None),
        P(("head", "blk"), None),
        P(("head", "blk"), None),
        P(("head", "blk"), None),
        P(("head", "blk"), None),
        P(("head", "blk"), None),
        P(("head", "blk"), None),
        P(("head", "blk")),
        P(("head", "blk")),
        P(),
        P(),
        P(("blk", "head"), None),
    )
    out_specs = (
        P(("blk", "head"), None),
        P(("blk", "head"), None),
        P(("head", "blk"), None),
        P(("head", "blk"), None),
        P(("head", "blk"), None),
        P(("head", "blk"), None),
        P(("head", "blk"), None),
        P(("head", "blk"), None),
        P(("head", "blk"), None),
        P(("head", "blk")),
        P(("head", "blk")),
        P(),
        P(),
    )
    return jax.shard_map(
        per_device, mesh=mesh, in_specs=in_specs, out_specs=out_specs, check_vma=False
    )
```

time: 1430 us -> 667 us (0.47)
  waiting for transfers between devices: 592 us -> 251 us
  matrix products: 237 us -> 46.5 us
  blocking collectives: 154 us -> 7.76 us
  starting transfers between devices: 237 us -> 96.8 us
  Pallas kernels: 0 us -> 97.1 us
  other arithmetic: 77.5 us -> 54.5 us
    reduce_scatter x11 -> x4, waiting for transfers between devices: 320 us -> 52.5 us  [the longest x2 51.4 us: to_owner(): lax.psum_scatter(regroup(grad), 'blk', scatter_dimension=0, tiled=True)]
    dot_general x49 -> x10, matrix products: 237 us -> 46.5 us  [dot(): return lax.dot_general(a, b, dims, preferred_element_type=F32)]
    all_gather x9 -> x3, waiting for transfers between devices: 176 us -> 0.02 us  [the longest x1 0.02 us: per_device(): qkv_ext = lax.all_gather(qkv_piece, 'blk', axis=1).reshape(depth, 640)]
    ppermute x32 -> x51, waiting for transfers between devices: 36.5 us -> 185 us  [permute(): return lax.ppermute(x, axis, [(i, move(i) % count) for i in range(count)])]
    ppermute x32 -> x51, starting transfers between devices: 196 us -> 77.6 us  [permute(): return lax.ppermute(x, axis, [(i, move(i) % count) for i in range(count)])]
    pallas_call x0 -> x10, Pallas kernels: none -> 97.1 us  [the longest x4 59.3 us: attend_back(): pl.pallas_call(body, out_shape=(jax.ShapeDtypeStruct(query.shape, F32), j...]
    all_gather x4 -> x0, blocking collectives: 70.3 us -> none  [the longest x1 19.6 us: per_device(): lax.all_gather(key_weight, 'blk', axis=0, tiled=True)]
    psum x1 -> x0, blocking collectives: 47.1 us -> none  [per_device(): lax.psum((query_gain_grad, key_gain_grad), ('head', 'blk'))]
  transfers between devices with their start and end apart: 65 -> 63, of which waited for: 41 -> 31; matrix products, arithmetic and copies ran while one was open for 14% -> 21% of each run, Pallas kernels for 0% -> 15%
where the time goes in v1:
time: 667 us; the launch traced here: 655 us
  waiting for transfers between devices  251 us (38%)
  Pallas kernels  97.1 us (15%)
  starting transfers between devices  96.8 us (15%)
  local copies, waits for them, and re-layouts  85.3 us (13%)
  other arithmetic  54.5 us (8%)
  matrix products  46.5 us (7%)
  between operations  16.1 us (2%)
  blocking collectives  7.76 us (1%)
    ppermute x51, waiting for transfers between devices, permute(): return lax.ppermute(x, axis, [(i, move(i) % count) for i in range(count)])  185 us
    ppermute x51, starting transfers between devices, permute(): return lax.ppermute(x, axis, [(i, move(i) % count) for i in range(count)])  77.6 us
    pallas_call x4, Pallas kernels, attend_back(): pl.pallas_call(body, out_shape=(jax.ShapeDtypeStruct(query.shape, F32), j...  59.3 us
    reduce_scatter x2, waiting for transfers between devices, to_owner(): lax.psum_scatter(regroup(grad), 'blk', scatter_dimension=0, tiled=True)  51.4 us
    dot_general x10, matrix products, dot(): return lax.dot_general(a, b, dims, preferred_element_type=F32)  46.5 us
    pallas_call x4, Pallas kernels, attend(): pl.pallas_call(body, out_shape=jax.ShapeDtypeStruct(query.shape, F32), in...  24.8 us
    dynamic_update_slice x23, local copies, waits for them, and re-layouts, gather_head(): lax.dynamic_update_slice(out, part, ((place ^ other) * rows + shift, 0))  21.4 us
    unnamed x144, local copies, waits for them, and re-layouts  17 us
  transfers between devices with their start and end apart: 63, of which 31 were waited for; matrix products, arithmetic and copies ran while one was open for 21% of the time, Pallas kernels for 15%

profile of v1, /device:TPU:9, one launch (start us, length us, event | category | flops | bytes accessed | tf_op | source)
XLA Modules:
  0.0 655.1 jit_solution(1149246607509735608)
XLA Ops:
  11.2 7.8 %all_to_all.58 = bf16[4,32,640]{2,1,0:T(8,128)(2,1)} all-to-all(bf16[4,32,640]{2,1,0:T(8,128)(2,1)S(1)} %maximum_bitcast_fusion.1), channel_id=1, replica_groups=mesh['head'=4,'blk'=8] {'head'}, dimensions={0} | all-to-all | bytes 327680 | tf_op jit(solution)/shard_map/all_to_all | solution.py:469
  23.4 23.0 %collective-permute-done = bf16[256,1024]{1,0:T(8,128)(2,1)S(1)} collective-permute-done((bf16[256,1024]{1,0:T(8,128)(2,1)S(1)}, bf16[256,1024]{1,0:T(8,128)(2,1)S(1)}, u32[]{:S(2)}, u32[]{:S(2)}) %collective-permute-start) | collective-permute-done | bytes 524320 | tf_op jit(solution)/shard_map/ppermute | solution.py:362
  91.7 41.2 %collective-permute-done.23 = bf16[256,1024]{1,0:T(8,128)(2,1)} collective-permute-done((bf16[256,1024]{1,0:T(8,128)(2,1)}, bf16[256,1024]{1,0:T(8,128)(2,1)}, u32[]{:S(2)}, u32[]{:S(2)}) %collective-permute-start.23) | collective-permute-done | bytes 524320 | tf_op jit(solution)/shard_map/ppermute | solution.py:362
  135.6 7.5 %shard_map.229.acc_ref = f32[2,2048,128]{2,1,0:T(8,128)S(1)} custom-call(s32[2]{0:T(128)S(1)} %add_multiply_fusion.3.off_ref, bf16[2,2048,128]{2,1,0:T(8,128)(2,1)S(1)} %pad_maximum_fusion.6.q_ref, bf16[2048,128]{1,0:T(8,128)(2,1)S(1)} %get-tuple-element.93.kv_ref), custom_call_target="tpu_custom_call" | custom-call | flops 4294967296 | bytes 8388608 | tf_op jit(solution)/shard_map/pallas_call | solution.py:102
  143.1 11.2 %collective-permute-done.7.kv_ref = bf16[2048,128]{1,0:T(8,128)(2,1)S(1)} collective-permute-done((bf16[2048,128]{1,0:T(8,128)(2,1)S(1)}, bf16[2048,128]{1,0:T(8,128)(2,1)S(1)}, u32[]{:S(2)}, u32[]{:S(2)}) %collective-permute-start.7) | collective-permute-done | bytes 524320 | tf_op jit(solution)/shard_map/ppermute | solution.py:362
  208.1 14.4 %collective-permute-done.12 = bf16[128,1024]{1,0:T(8,128)(2,1)S(1)} collective-permute-done((bf16[128,1024]{1,0:T(8,128)(2,1)S(1)}, bf16[128,1024]{1,0:T(8,128)(2,1)S(1)}, u32[]{:S(2)}, u32[]{:S(2)}) %collective-permute-start.12) | collective-permute-done | bytes 262176 | tf_op jit(solution)/shard_map/ppermute | solution.py:362
  236.6 10.5 %collective-permute-done.27 = bf16[128,1024]{1,0:T(8,128)(2,1)S(1)} collective-permute-done((bf16[128,1024]{1,0:T(8,128)(2,1)S(1)}, bf16[128,1024]{1,0:T(8,128)(2,1)S(1)}, u32[]{:S(2)}, u32[]{:S(2)}) %collective-permute-start.27) | collective-permute-done | bytes 262176 | tf_op jit(solution)/shard_map/ppermute | solution.py:362
  273.2 7.4 %fusion.2 = (bf16[1024,1152]{1,0:T(8,128)(2,1)S(1)}, bf16[1024,1152]{1,0:T(8,128)(2,1)S(1)}, bf16[1024,1152]{1,0:T(8,128)(2,1)S(1)}) fusion(bf16[1024,1152]{1,0:T(8,128)(2,1)S(1)} %copy-done.67, f32[1024,1152]{1,0:T(8,128)S(1)} %fusion.8, bf16[1024,1024]{1,0:T(8,128)(2,1)} %constant_dynamic-update-slice_fusion.10, bf16[1024,2304]{1,0:T(8,128)(2,1)S(1)} %bitcast.123), kind=kOutput, calls=%fused_computation.5 | convolution fusion | flops 2435973120 | bytes 18612224 | tf_op jit(solution)/shard_map/dot_general | solution.py:29
  297.2 8.3 %collective-permute-done.28 = bf16[256,1024]{1,0:T(8,128)(2,1)} collective-permute-done((bf16[256,1024]{1,0:T(8,128)(2,1)}, bf16[256,1024]{1,0:T(8,128)(2,1)}, u32[]{:S(2)}, u32[]{:S(2)}) %collective-permute-start.28) | collective-permute-done | bytes 524320 | tf_op jit(solution)/shard_map/ppermute | solution.py:362
  349.9 10.4 %collective-permute-start.32 = (bf16[1024,128]{1,0:T(8,128)(2,1)S(1)}, bf16[1024,128]{1,0:T(8,128)(2,1)S(1)}, u32[]{:S(2)}, u32[]{:S(2)}) collective-permute-start(bf16[1024,128]{1,0:T(8,128)(2,1)S(1)} %broadcast_select_fusion.3), channel_id=1, source_target_pairs={{0,1},{1,0},{2,3},{3,2},{4,5},{5,4},{6,7},{7,6},{8,9},{9,8},{10,11... | collective-permute-start | bytes 786440 | tf_op jit(solution)/shard_map/ppermute | solution.py:362
  381.7 6.3 concatenate.82.do_ref
  388.0 16.8 %shard_map.236 = (f32[2,2048,128]{2,1,0:T(8,128)S(1)}, f32[2048,128]{1,0:T(8,128)S(1)}) custom-call(s32[2]{0:T(128)S(1)} %add_multiply_fusion.3.off_ref, bf16[2,2048,128]{2,1,0:T(8,128)(2,1)S(1)} %pad_maximum_fusion.6.q_ref, bf16[2,2048,128]{2,1,0:T(8,128)(2,1)S(1)} %concatenate.82.do_ref, bf16[2048,128]{1,0:T(8,128)(2,1)S(1)} %copy-done.3), custom_call_target="tpu_custom_call" | custom-call | flops 10737418240 | bytes 8388608 | tf_op jit(solution)/shard_map/pallas_call | solution.py:196
  406.3 14.0 %shard_map.233 = (f32[2,2048,128]{2,1,0:T(8,128)S(1)}, f32[2048,128]{1,0:T(8,128)S(1)}) custom-call(s32[4]{0:T(128)S(1)} %add_multiply_fusion.2.off_ref, bf16[2,2048,128]{2,1,0:T(8,128)(2,1)S(1)} %pad_maximum_fusion.6.q_ref, bf16[2,2048,128]{2,1,0:T(8,128)(2,1)S(1)} %concatenate.82.do_ref, bf16[2048,128]{1,0:T(8,128)(2,1)S(1)} %copy-done.11, ...), custom_call_target="tpu_custom_call" | custom-call | flops 10737418240 | bytes 8388608 | tf_op jit(solution)/shard_map/pallas_call | solution.py:196
  421.7 14.2 %shard_map.234 = (f32[2,2048,128]{2,1,0:T(8,128)S(1)}, f32[2048,128]{1,0:T(8,128)S(1)}) custom-call(s32[4]{0:T(128)S(1)} %get-tuple-element.110.off_ref, bf16[2,2048,128]{2,1,0:T(8,128)(2,1)S(1)} %pad_maximum_fusion.6.q_ref, bf16[2,2048,128]{2,1,0:T(8,128)(2,1)S(1)} %concatenate.82.do_ref, bf16[2048,128]{1,0:T(8,128)(2,1)S(1)} %copy-done.15, ...), custom_call_target="tpu_custom_call" | custom-call | flops 10737418240 | bytes 8388608 | tf_op jit(solution)/shard_map/pallas_call | solution.py:196
  437.6 14.3 %shard_map.235 = (f32[2,2048,128]{2,1,0:T(8,128)S(1)}, f32[2048,128]{1,0:T(8,128)S(1)}) custom-call(s32[4]{0:T(128)S(1)} %get-tuple-element.109.off_ref, bf16[2,2048,128]{2,1,0:T(8,128)(2,1)S(1)} %pad_maximum_fusion.6.q_ref, bf16[2,2048,128]{2,1,0:T(8,128)(2,1)S(1)} %concatenate.82.do_ref, bf16[2048,128]{1,0:T(8,128)(2,1)S(1)} %copy-done.13, ...), custom_call_target="tpu_custom_call" | custom-call | flops 10737418240 | bytes 8388608 | tf_op jit(solution)/shard_map/pallas_call | solution.py:196
  461.1 6.6 %collective-permute-start.36 = (bf16[1024,256]{1,0:T(8,128)(2,1)S(1)}, bf16[1024,256]{1,0:T(8,128)(2,1)}, u32[]{:S(2)}, u32[]{:S(2)}) collective-permute-start(bf16[1024,256]{1,0:T(8,128)(2,1)S(1)} %broadcast_select_fusion.1), channel_id=1, source_target_pairs={{0,1},{1,0},{2,3},{3,2},{4,5},{5,4},{6,7},{7,6},{8,9},{9,8},{10,11... | collective-permute-start | bytes 1572872 | tf_op jit(solution)/shard_map/ppermute | solution.py:362
  473.2 8.2 %shard_map.237 = (bf16[1024,1024]{1,0:T(8,128)(2,1)S(1)}, bf16[1024,512]{1,0:T(8,128)(2,1)S(1)}, f32[8,128]{1,0:T(8,128)S(1)}) custom-call(f32[1024,512]{1,0:T(8,128)S(1)} %copy-done.19, bf16[2,1024,256]{2,1,0:T(8,128)(2,1)S(1)} %pad_maximum_fusion.8.grad_ref, bf16[1024,1024]{1,0:T(8,128)(2,1)S(1)} %copy-done.17, bf16[1024,512]{1,0:T(8,128)(2,1)S(1)} %copy-done.1, ...), custom_call_target="tpu_custom_call" | custom-call | flops 4294967296 | bytes 8388608 | tf_op jit(solution)/shard_map/pallas_call | solution.py:330
  482.8 6.4 convolution_convert_fusion.1
  489.2 8.1 %convolution_convert_fusion = bf16[1024,2304]{1,0:T(8,128)(2,1)S(1)} fusion(bf16[1024,1024]{1,0:T(8,128)(2,1)} %constant_dynamic-update-slice_fusion.10, bf16[1024,1152]{1,0:T(8,128)(2,1)} %copy-done.65, bf16[1024,1152]{1,0:T(8,128)(2,1)} %copy-done.64), kind=kOutput, calls=%fused_computation.2 | convolution fusion | flops 4843634688 | bytes 11534336 | tf_op jit(solution)/shard_map/dot_general | solution.py:29
  501.6 12.0 %collective-permute-done.37 = bf16[256,1024]{1,0:T(8,128)(2,1)S(1)} collective-permute-done((bf16[256,1024]{1,0:T(8,128)(2,1)S(1)}, bf16[256,1024]{1,0:T(8,128)(2,1)S(1)}, u32[]{:S(2)}, u32[]{:S(2)}) %collective-permute-start.37) | collective-permute-done | bytes 524320 | tf_op jit(solution)/shard_map/ppermute | solution.py:362
  514.8 6.2 collective-permute-done.38
  545.5 9.0 %collective-permute-done.22 = bf16[256,1024]{1,0:T(8,128)(2,1)S(1)} collective-permute-done((bf16[256,1024]{1,0:T(8,128)(2,1)S(1)}, bf16[256,1024]{1,0:T(8,128)(2,1)S(1)}, u32[]{:S(2)}, u32[]{:S(2)}) %collective-permute-start.22) | collective-permute-done | bytes 524320 | tf_op jit(solution)/shard_map/ppermute | solution.py:362
  556.0 15.4 %collective-permute-done.50 = f32[2,128]{1,0:T(2,128)S(1)} collective-permute-done((f32[2,128]{1,0:T(2,128)S(1)}, f32[2,128]{1,0:T(2,128)S(1)}, u32[]{:S(2)}, u32[]{:S(2)}) %collective-permute-start.50) | collective-permute-done | bytes 1056 | tf_op jit(solution)/shard_map/ppermute | solution.py:362
  578.8 51.4 %reduce-scatter.9.cloned.1.call-done = bf16[128,2304]{1,0:T(8,128)(2,1)} async-done(((bf16[1024,2304]{1,0:T(8,128)(2,1)}), bf16[128,2304]{1,0:T(8,128)(2,1)}) %reduce-scatter.9.cloned.1.call-update) | async-done | bytes 589840 | tf_op jit(solution)/shard_map/reduce_scatter | solution.py:596
  (441 shorter events, 308.7 us)
Async XLA Ops:
  7.3 54.0 %all-gather.7.cloned.1.call-start = ((), (), s32[]{:S(2)}) async-start(), calls=%async_computation.14 | async-start | bytes 1474560 | tf_op jit(solution)/shard_map/all_gather | solution.py:474
  19.0 157.5 %all-gather.9.cloned.1.call-start = ((), (), s32[]{:S(2)}) async-start(), calls=%async_computation.15 | async-start | bytes 3244032 | tf_op jit(solution)/shard_map/all_gather | solution.py:450
  19.9 26.5 %collective-permute-start = (bf16[256,1024]{1,0:T(8,128)(2,1)S(1)}, bf16[256,1024]{1,0:T(8,128)(2,1)S(1)}, u32[]{:S(2)}, u32[]{:S(2)}) collective-permute-start(bf16[256,1024]{1,0:T(8,128)(2,1)S(1)} %copy-done.59), channel_id=1, source_target_pairs={{0,0},{1,7},{2,2},{3,5},{4,4},{5,3},{6,6},{7,1},{8,8},{9,15},{10,1... | collective-permute-start | bytes 1572872 | tf_op jit(solution)/shard_map/ppermute | solution.py:362
  78.8 186.8 %all-gather.11.cloned.1.call-start = ((), (), s32[]{:S(2)}) async-start(), calls=%async_computation.16 | async-start | bytes 5308416 | tf_op jit(solution)/shard_map/all_gather | solution.py:478
  78.9 53.9 %collective-permute-start.23 = (bf16[256,1024]{1,0:T(8,128)(2,1)}, bf16[256,1024]{1,0:T(8,128)(2,1)}, u32[]{:S(2)}, u32[]{:S(2)}) collective-permute-start(bf16[256,1024]{1,0:T(8,128)(2,1)} %param.25), channel_id=1, source_target_pairs={{0,0},{1,7},{2,2},{3,5},{4,4},{5,3},{6,6},{7,1},{8,8},{9,15},{10,1... | collective-permute-start | bytes 1572872 | tf_op jit(solution)/shard_map/ppermute | solution.py:362
  89.9 45.5 %collective-permute-start.6 = (bf16[2048,128]{1,0:T(8,128)(2,1)S(1)}, bf16[2048,128]{1,0:T(8,128)(2,1)S(1)}, u32[]{:S(2)}, u32[]{:S(2)}) collective-permute-start(bf16[2048,128]{1,0:T(8,128)(2,1)S(1)} %get-tuple-element.93.kv_ref), channel_id=1, source_target_pairs={{0,2},{1,3},{2,4},{3,5},{4,6},{5,7},{6,0},{7,1},{8,10},{9,11},{10,... | collective-permute-start | bytes 1572872 | tf_op jit(solution)/shard_map/ppermute | solution.py:362
  132.8 49.9 %collective-permute-start.24 = (bf16[256,1024]{1,0:T(8,128)(2,1)}, bf16[256,1024]{1,0:T(8,128)(2,1)}, u32[]{:S(2)}, u32[]{:S(2)}) collective-permute-start(bf16[256,1024]{1,0:T(8,128)(2,1)} %collective-permute-done.23), channel_id=1, source_target_pairs={{0,8},{8,0},{16,24},{24,16},{1,9},{9,1},{17,25},{25,17},{2,10},{10... | collective-permute-start | bytes 1572872 | tf_op jit(solution)/shard_map/ppermute | solution.py:362
  180.5 21.7 %collective-permute-start.11 = (bf16[256,1024]{1,0:T(8,128)(2,1)}, bf16[256,1024]{1,0:T(8,128)(2,1)}, u32[]{:S(2)}, u32[]{:S(2)}) collective-permute-start(bf16[256,1024]{1,0:T(8,128)(2,1)} %bitcast.28), channel_id=1, source_target_pairs={{0,16},{8,24},{16,0},{24,8},{1,17},{9,25},{17,1},{25,9},{2,18},{10... | collective-permute-start | bytes 1572872 | tf_op jit(solution)/shard_map/ppermute | solution.py:362
  182.7 48.3 %collective-permute-start.25 = (bf16[256,1024]{1,0:T(8,128)(2,1)}, bf16[256,1024]{1,0:T(8,128)(2,1)}, u32[]{:S(2)}, u32[]{:S(2)}) collective-permute-start(bf16[256,1024]{1,0:T(8,128)(2,1)} %collective-permute-done.23), channel_id=1, source_target_pairs={{0,16},{8,24},{16,0},{24,8},{1,17},{9,25},{17,1},{25,9},{2,18},{10... | collective-permute-start | bytes 1572872 | tf_op jit(solution)/shard_map/ppermute | solution.py:362
  184.4 51.2 %collective-permute-start.26 = (bf16[128,1024]{1,0:T(8,128)(2,1)}, bf16[128,1024]{1,0:T(8,128)(2,1)}, u32[]{:S(2)}, u32[]{:S(2)}) collective-permute-start(bf16[128,1024]{1,0:T(8,128)(2,1)} %slice.255), channel_id=1, source_target_pairs={{0,16},{8,24},{16,0},{24,8},{1,17},{9,25},{17,1},{25,9},{2,18},{10... | collective-permute-start | bytes 786440 | tf_op jit(solution)/shard_map/ppermute | solution.py:362
  191.9 32.2 %all-to-all-start.1 = ((bf16[4,256,256]{1,2,0:T(8,128)(2,1)}), bf16[4,256,256]{1,2,0:T(8,128)(2,1)}, u32[]{:S(2)}, u32[]{:S(2)}) async-start(bf16[4,256,256]{1,2,0:T(8,128)(2,1)} %copy.70), calls=%async_computation.1 | async-start | bytes 1048576 | tf_op jit(solution)/shard_map/all_to_all | solution.py:563
  197.2 25.4 %collective-permute-start.12 = (bf16[128,1024]{1,0:T(8,128)(2,1)S(1)}, bf16[128,1024]{1,0:T(8,128)(2,1)S(1)}, u32[]{:S(2)}, u32[]{:S(2)}) collective-permute-start(bf16[128,1024]{1,0:T(8,128)(2,1)S(1)} %slice.243), channel_id=1, source_target_pairs={{0,16},{8,24},{16,0},{24,8},{1,17},{9,25},{17,1},{25,9},{2,18},{10... | collective-permute-start | bytes 786440 | tf_op jit(solution)/shard_map/ppermute | solution.py:362
  203.2 20.1 %collective-permute-start.13 = (bf16[128,1024]{1,0:T(8,128)(2,1)S(1)}, bf16[128,1024]{1,0:T(8,128)(2,1)S(1)}, u32[]{:S(2)}, u32[]{:S(2)}) collective-permute-start(bf16[128,1024]{1,0:T(8,128)(2,1)S(1)} %slice.244), channel_id=1, source_target_pairs={{0,8},{8,0},{16,24},{24,16},{1,9},{9,1},{17,25},{25,17},{2,10},{10... | collective-permute-start | bytes 786440 | tf_op jit(solution)/shard_map/ppermute | solution.py:362
  296.9 19.7 %collective-permute-start.19 = (bf16[128,1024]{1,0:T(8,128)(2,1)}, bf16[128,1024]{1,0:T(8,128)(2,1)}, u32[]{:S(2)}, u32[]{:S(2)}) collective-permute-start(bf16[128,1024]{1,0:T(8,128)(2,1)} %fusion.39), channel_id=1, source_target_pairs={{0,16},{8,24},{16,0},{24,8},{1,17},{9,25},{17,1},{25,9},{2,18},{10... | collective-permute-start | bytes 786440 | tf_op jit(solution)/shard_map/ppermute | solution.py:362
  343.3 211.2 %reduce-scatter.7.cloned.1.call-start = ((), (), s32[]{:S(2)}) async-start(), calls=%async_computation.11 | async-start | bytes 589824 | tf_op jit(solution)/shard_map/reduce_scatter | solution.py:613
  349.9 19.0 %collective-permute-start.32 = (bf16[1024,128]{1,0:T(8,128)(2,1)S(1)}, bf16[1024,128]{1,0:T(8,128)(2,1)S(1)}, u32[]{:S(2)}, u32[]{:S(2)}) collective-permute-start(bf16[1024,128]{1,0:T(8,128)(2,1)S(1)} %broadcast_select_fusion.3), channel_id=1, source_target_pairs={{0,1},{1,0},{2,3},{3,2},{4,5},{5,4},{6,7},{7,6},{8,9},{9,8},{10,11... | collective-permute-start | bytes 786440 | tf_op jit(solution)/shard_map/ppermute | solution.py:362
  361.9 93.2 %collective-permute-start.44 = (bf16[128,1024]{1,0:T(8,128)(2,1)}, bf16[128,1024]{1,0:T(8,128)(2,1)}, u32[]{:S(2)}, u32[]{:S(2)}) collective-permute-start(bf16[128,1024]{1,0:T(8,128)(2,1)} %slice.276), channel_id=1, source_target_pairs={{0,16},{8,24},{16,0},{24,8},{1,17},{9,25},{17,1},{25,9},{2,18},{10... | collective-permute-start | bytes 786440 | tf_op jit(solution)/shard_map/ppermute | solution.py:362
  364.8 92.5 %collective-permute-start.45 = (bf16[128,1024]{1,0:T(8,128)(2,1)}, bf16[128,1024]{1,0:T(8,128)(2,1)}, u32[]{:S(2)}, u32[]{:S(2)}) collective-permute-start(bf16[128,1024]{1,0:T(8,128)(2,1)} %slice.277), channel_id=1, source_target_pairs={{0,8},{8,0},{16,24},{24,16},{1,9},{9,1},{17,25},{25,17},{2,10},{10... | collective-permute-start | bytes 786440 | tf_op jit(solution)/shard_map/ppermute | solution.py:362
  469.2 102.2 %reduce-scatter.5.cloned.1.call-start = ((), (), s32[]{:S(2)}) async-start(), calls=%async_computation.10 | async-start | bytes 1179648 | tf_op jit(solution)/shard_map/reduce_scatter | solution.py:596
  482.5 93.8 %reduce-scatter.11.cloned.1.call-start = ((), (), s32[]{:S(2)}) async-start(), calls=%async_computation.13 | async-start | bytes 2654208 | tf_op jit(solution)/shard_map/reduce_scatter | solution.py:586
  489.1 141.0 %reduce-scatter.9.cloned.1.call-start = ((), (), s32[]{:S(2)}) async-start(), calls=%async_computation.12 | async-start | bytes 5308416 | tf_op jit(solution)/shard_map/reduce_scatter | solution.py:596
  522.6 31.9 %collective-permute-start.22 = (bf16[256,1024]{1,0:T(8,128)(2,1)S(1)}, bf16[256,1024]{1,0:T(8,128)(2,1)S(1)}, u32[]{:S(2)}, u32[]{:S(2)}) collective-permute-start(bf16[256,1024]{1,0:T(8,128)(2,1)S(1)} %copy-done.51), channel_id=1, source_target_pairs={{0,0},{1,7},{2,2},{3,5},{4,4},{5,3},{6,6},{7,1},{8,8},{9,15},{10,1... | collective-permute-start | bytes 1572872 | tf_op jit(solution)/shard_map/ppermute | solution.py:362
  528.4 49.8 %collective-permute-start.41 = (bf16[256,1024]{1,0:T(8,128)(2,1)S(1)}, bf16[256,1024]{1,0:T(8,128)(2,1)S(1)}, u32[]{:S(2)}, u32[]{:S(2)}) collective-permute-start(bf16[256,1024]{1,0:T(8,128)(2,1)S(1)} %fusion.21), channel_id=1, source_target_pairs={{0,0},{1,7},{2,2},{3,5},{4,4},{5,3},{6,6},{7,1},{8,8},{9,15},{10,1... | collective-permute-start | bytes 1572872 | tf_op jit(solution)/shard_map/ppermute | solution.py:362
  543.4 28.0 %collective-permute-start.50 = (f32[2,128]{1,0:T(2,128)S(1)}, f32[2,128]{1,0:T(2,128)S(1)}, u32[]{:S(2)}, u32[]{:S(2)}) collective-permute-start(f32[2,128]{1,0:T(2,128)S(1)} %add.336), channel_id=1, source_target_pairs={{0,4},{1,5},{2,6},{3,7},{4,0},{5,1},{6,2},{7,3},{8,12},{9,13},{10,... | collective-permute-start | bytes 3080 | tf_op jit(solution)/shard_map/ppermute | solution.py:362
  (107 other events, 1060.3 us)
Sparse Core Ops, SparseCore 0:
  19.1 28.7 all-gather.6
  49.6 36.1 all-gather.8
  89.2 65.3 all-gather.10
  469.3 24.5 reduce-scatter.6
  496.1 30.7 reduce-scatter.4
  529.3 47.0 reduce-scatter.10
  578.8 51.3 reduce-scatter.8

commit v2 on v1

v2 whole, which is shorter than its diff:
```python
import functools
import math

import jax
import jax.numpy as jnp
from jax import lax
from jax.experimental import pallas as pl
from jax.experimental.pallas import tpu as pltpu
from jax.sharding import PartitionSpec as P

HQ = 16
KV = 8
HD = 64
EPSILON = 1e-05
ROPE_BASE = 1000000.0
TILE = 1024
QUERY_UNIT = math.log2(math.e) * HD**-0.5

BF = jnp.bfloat16
F32 = jnp.float32
NT = (((1,), (1,)), ((), ()))
NN = (((1,), (0,)), ((), ()))
TN = (((0,), (0,)), ((), ()))
VM = pl.BlockSpec(memory_space=pltpu.VMEM)
SM = pl.BlockSpec(memory_space=pltpu.SMEM)


def dot(a, b, dims=NN):
    return lax.dot_general(a, b, dims, preferred_element_type=F32)


def run(body, outs, args, flops=0, scalars=None, scratch=(), exps=0, limit=40, far=(), stay=()):
    args = list(args)
    hbm = pl.BlockSpec(memory_space=pltpu.HBM)
    specs = [hbm if i in far or i in stay else VM for i in range(len(args))]
    many = isinstance(outs, (list, tuple))
    outs = list(outs) if many else [outs]
    size = sum(math.prod(a.shape) * a.dtype.itemsize for a in outs + args)
    scratch = list(scratch)
    if far:
        own, lead = len(scratch), 0 if scalars is None else 1
        scratch += [pltpu.VMEM(args[i].shape, args[i].dtype) for i in far]
        scratch.append(pltpu.SemaphoreType.DMA((len(far),)))
        inner = body

        def body(*refs):
            refs = list(refs)
            sems = refs.pop()
            buffers = refs[-len(far) :]
            refs = refs[: -len(far)]
            copies = [
                pltpu.make_async_copy(refs[lead + i], buffer, sems.at[k])
                for k, (i, buffer) in enumerate(zip(far, buffers, strict=True))
            ]
            for copy in copies:
                copy.start()
            for copy in copies:
                copy.wait()
            for i, buffer in zip(far, buffers, strict=True):
                refs[lead + i] = buffer
            inner(*refs)

    if scalars is not None:
        args = [jnp.stack([jnp.asarray(v, jnp.int32) for v in scalars])] + args
        specs = [SM] + specs
    return pl.pallas_call(
        body,
        out_shape=tuple(outs) if many else outs[0],
        in_specs=specs,
        out_specs=tuple([VM] * len(outs)) if many else VM,
        scratch_shapes=scratch,
        cost_estimate=pl.CostEstimate(flops=1, bytes_accessed=1, transcendentals=0),
        compiler_params=pltpu.CompilerParams(vmem_limit_bytes=60 << 20),
    )(*args)


def shape(*dims, dtype=BF):
    return jax.ShapeDtypeStruct(dims, dtype)


def pair_list(off_ref, span, count):
    return [
        (pl.multiple_of(off_ref[2 * i], span), pl.multiple_of(off_ref[2 * i + 1], span))
        for i in range(count)
    ]


def attend_body(span, heads, local, first, last, off_ref, q_ref, kv_ref, *refs):
    refs = list(refs)
    acc_ref = None if first else refs.pop(0)
    out_ref = refs.pop(0)
    mix_ref = refs.pop(0) if last else None
    ones_ref = refs.pop(0)
    lane = lax.broadcasted_iota(jnp.int32, ones_ref.shape, 1)
    ones_ref[...] = jnp.where(lane < HD, jnp.ones((), BF), kv_ref[...])
    out_ref[...] = jnp.zeros_like(out_ref) if first else acc_ref[...]
    block = min(span, TILE)

    def block_pair(head, q_off, k_off):
        rows = pl.ds(q_off, block)
        keys = pl.ds(k_off, block)
        query = q_ref[rows, 128 * head : 128 * head + 128]
        weight = jnp.exp2(dot(query, kv_ref[keys, :], NT)).astype(BF)
        out_ref[head, rows, :] += dot(weight, ones_ref[keys, :])

    def full(q_off, k_off):
        for i in range(span // block):
            for j in range(span // block):
                for head in range(heads):
                    block_pair(head, q_off + i * block, k_off + j * block)

    def diagonal(start):
        for i in range(span // block):
            for j in range(i):
                for head in range(heads):
                    block_pair(head, start + i * block, start + j * block)
            diagonal_block(start + i * block)

    def diagonal_block(start):
        size = 256
        for head in range(heads):
            for i in range(block // size):
                rows = slice(start + i * size, start + (i + 1) * size)
                query = q_ref[rows, 128 * head : 128 * head + 128]
                total = None
                pieces = ([(0, i * size)] if i else []) + [(i * size, (i + 1) * size)]
                for low, high in pieces:
                    keys = slice(start + low, start + high)
                    weight = jnp.exp2(dot(query, kv_ref[keys, :], NT))
                    if low == i * size:
                        place = lax.broadcasted_iota(jnp.int32, (size, size), 0)
                        other = lax.broadcasted_iota(jnp.int32, (size, size), 1)
                        weight = jnp.where(other <= place, weight, 0.0)
                    part = dot(weight.astype(BF), ones_ref[keys, :])
                    total = part if total is None else total + part
                out_ref[head, rows, :] += total

    if local:
        diagonal(0)
        diagonal(span)
    for q_off, k_off in pair_list(off_ref, span, 1 if local else 2):
        full(q_off, k_off)
    if last:
        size = 256
        for i in range(2 * span // size):
            rows = slice(i * size, (i + 1) * size)
            left = lax.broadcasted_iota(jnp.int32, (size, 2 * HD), 1) < HD
            mixed = []
            for head in range(heads):
                total = out_ref[head, rows, :]
                mixed.append(total * pltpu.roll(1.0 / jnp.where(left, total, 1.0), HD, 1))
            out = jnp.where(left, pltpu.roll(mixed[0], HD, 1), mixed[1] if heads > 1 else 0.0)
            mix_ref[i * size // span, pl.ds(i * size % span, size), :] = out.astype(BF)


def attend(offsets, packets, kv, acc, local, last, heads):
    span = packets.shape[0] // 2
    outs = [shape(heads, 2 * span, 2 * HD, dtype=F32)]
    if last:
        outs.append(shape(2, span, 2 * HD))
    return run(
        functools.partial(attend_body, span, heads, local, acc is None, last),
        outs,
        [packets, kv] + ([] if acc is None else [acc]),
        flops=8 * heads * span * span * 256,
        scalars=offsets,
        scratch=[pltpu.VMEM((2 * span, 2 * HD), BF)],
        exps=2 * heads * span * span,
        far=() if local else (0,),
    )


def attend_back_body(
    span, heads, local, first, off_ref, q_ref, do_ref, kv_ref, *refs
):
    refs = list(refs)
    acc_ref = None if first else refs.pop(0)
    if local:
        dq_ref, dkv_ref, ones_ref, dv_ref = refs
    else:
        dq_ref, out_ref, ones_ref, dv_ref, dkv_ref = refs
    lane = lax.broadcasted_iota(jnp.int32, ones_ref.shape, 1)
    zero = jnp.zeros((), BF)
    ones_ref[...] = jnp.where(
        lane < HD, jnp.where(lane < 3, jnp.ones((), BF), zero), kv_ref[...]
    )
    block = min(span, TILE)
    for head in range(heads):
        dv_ref[head] = jnp.where(lane < HD, zero, do_ref[head])
    dq_ref[...] = jnp.zeros_like(dq_ref) if first else acc_ref[...]
    dkv_ref[...] = jnp.zeros_like(dkv_ref)

    def tile(head, rows, keys, mask):
        query = q_ref[rows, 128 * head : 128 * head + 128]
        pair = kv_ref[keys, :]
        weight = jnp.exp2(dot(pair, query, NT))
        if mask is not None:
            weight = jnp.where(mask, weight, 0.0)
        score_grad = (weight * dot(ones_ref[keys, :], do_ref[head, rows, :], NT)).astype(BF)
        dkv_ref[keys, :] += dot(weight.astype(BF), dv_ref[head, rows, :]) + dot(score_grad, query)
        dq_ref[head, rows, :] += dot(score_grad, pair, TN)

    def block_pair(head, q_off, k_off):
        tile(head, pl.ds(q_off, block), pl.ds(k_off, block), None)

    def full(q_off, k_off):
        for i in range(span // block):
            for j in range(span // block):
                for head in range(heads):
                    block_pair(head, q_off + i * block, k_off + j * block)

    def diagonal(start):
        for i in range(span // block):
            for j in range(i):
                for head in range(heads):
                    block_pair(head, start + i * block, start + j * block)
            diagonal_block(start + i * block)

    def diagonal_block(start):
        size = 256
        for head in range(heads):
            for i in range(block // size):
                rows = slice(start + i * size, start + (i + 1) * size)
                pieces = ([(0, i * size)] if i else []) + [(i * size, (i + 1) * size)]
                for low, high in pieces:
                    mask = None
                    if low == i * size:
                        key_place = lax.broadcasted_iota(jnp.int32, (size, size), 0)
                        mask = key_place <= lax.broadcasted_iota(jnp.int32, (size, size), 1)
                    tile(head, rows, slice(start + low, start + high), mask)

    if local:
        diagonal(0)
        diagonal(span)
    for q_off, k_off in pair_list(off_ref, span, 1 if local else 2):
        full(q_off, k_off)
    if not local:
        out_ref[...] = dkv_ref[...].astype(BF)


def attend_back(offsets, packets, out_grad, kv, acc, local):
    heads, rows = out_grad.shape[:2]
    span = rows // 2
    return run(
        functools.partial(attend_back_body, span, heads, local, acc is None),
        [shape(heads, rows, 2 * HD, dtype=F32), shape(rows, 2 * HD, dtype=F32 if local else BF)],
        [packets, out_grad, kv] + ([] if acc is None else [acc]),
        flops=20 * heads * span * span * 256,
        scalars=offsets,
        scratch=[pltpu.VMEM((rows, 2 * HD), BF), pltpu.VMEM((heads, rows, 2 * HD), BF)]
        + ([] if local else [pltpu.VMEM((rows, 2 * HD), F32)]),
        exps=2 * heads * span * span,
        limit=48,
        far=(0, 2),
    )


def out_grad_body(core_ref, mine_ref, theirs_ref, acc_ref, out_ref):
    heads, rows = acc_ref.shape[:2]
    size = 256
    lane = lax.broadcasted_iota(jnp.int32, (size, 2 * HD), 1)
    left = lane < HD
    for i in range(rows // size):
        here = slice(i * size, (i + 1) * size)
        if i * size < rows // 2:
            first = mine_ref[here, 0:128]
            second = mine_ref[here, 128:256]
            both = jnp.where(core_ref[0] == 0, first, second).astype(F32)
        else:
            both = theirs_ref[slice(i * size - rows // 2, (i + 1) * size - rows // 2), :].astype(F32)
        for head in range(heads):
            grad = pltpu.roll(both, HD, 1) if head == 0 else both
            total = acc_ref[head, here, :]
            inverse = pltpu.roll(1.0 / jnp.where(left, total, 1.0), HD, 1)
            scaled = grad * inverse
            delta = jnp.sum(
                jnp.where(left, 0.0, scaled * total * inverse), axis=1, keepdims=True
            )
            shift = jnp.broadcast_to(-delta, (size, 2 * HD))
            high = shift.astype(BF).astype(F32)
            rest = shift - high
            middle = rest.astype(BF).astype(F32)
            parts = jnp.where(lane == 0, high, jnp.where(lane == 1, middle, rest - middle))
            out = jnp.where(left, jnp.where(lane < 3, parts, 0.0), scaled)
            out_ref[head, here, :] = out.astype(BF)


def pack_body(dq_ref, dkv_ref, *refs):
    outs = refs[-2:]
    heads, rows = dq_ref.shape[:2]
    span = rows // 2
    size = 256
    lane = lax.broadcasted_iota(jnp.int32, (size, 2 * HD), 1)
    for i in range(rows // size):
        here = slice(i * size, (i + 1) * size)
        there = slice(i * size % span, i * size % span + size)
        out = outs[i * size // span]
        query = dq_ref[0, here, :]
        other = pltpu.roll(dq_ref[1, here, :], HD, 1) if heads > 1 else 0.0
        query = jnp.where(lane < HD, query, other) * (HD**-0.5)
        pair = dkv_ref[here, :]
        for more in refs[:-2]:
            pair = pair + more[here, :].astype(F32)
        pair = pair * jnp.where(lane < HD, math.log(2.0), 1.0)
        out[there, 0:128] = query.astype(BF)
        out[there, 128:256] = pair.astype(BF)


def swap_halves(x):
    lane = lax.broadcasted_iota(jnp.int32, x.shape, 1)
    return jnp.where(
        lane % HD < HD // 2, pltpu.roll(x, x.shape[1] - HD // 2, 1), pltpu.roll(x, HD // 2, 1)
    )


def head_mean(x):
    size = x.shape[1]
    first = lax.broadcasted_iota(jnp.int32, (size, size), 0) // HD
    second = lax.broadcasted_iota(jnp.int32, (size, size), 1) // HD
    ones = jnp.where(first == second, 1.0 / HD, 0.0).astype(BF)
    high = x.astype(BF)
    low = (x - high.astype(F32)).astype(BF)
    return dot(high, ones) + dot(low, ones)


def unit_norm(x):
    return x * lax.rsqrt(jnp.mean(x * x, axis=1, keepdims=True) + EPSILON)


def tiles_of(refs, size=256):
    for k, ref in enumerate(refs):
        step = min(size, ref.shape[0])
        for low in range(0, ref.shape[0], step):
            yield k, low, step


def assemble_body(heads, index_ref, mine_ref, theirs_ref, out_ref):
    count = mine_ref.shape[0]
    for r in range(count):
        for h in range(heads):
            row = index_ref[2 * count + h]
            out_ref[row, index_ref[r]] = mine_ref[r, h]
            out_ref[row, index_ref[count + r]] = theirs_ref[r, h]


def project_body(count, heads, at_ref, *refs):
    x_refs = refs[:count]
    w_ref, cos_ref, sin_ref, head_gain_ref, keep_ref, send_ref, rows_ref = refs[count:]
    core = at_ref[count]
    rows_ref[...] = w_ref[:, 512:640].astype(F32).T[0:8]
    gain = rows_ref[0:1, :]
    for k, low, size in tiles_of(x_refs):
        start = pl.ds(pl.multiple_of(at_ref[k] + low, 128), size)
        normed = (unit_norm(x_refs[k][low : low + size, :].astype(F32)) * gain).astype(BF)
        cosine, sine = cos_ref[start, :], sin_ref[start, :]
        lane = lax.broadcasted_iota(jnp.int32, cosine.shape, 1)
        for unit, out_ref in ((core, keep_ref), (1 - core, send_ref)):
            raw = dot(normed, w_ref[:, pl.ds(pl.multiple_of(256 * unit, 256), 256)])
            query, pair = raw[:, :128], raw[:, 128:]
            query = query * lax.rsqrt(head_mean(query * query) + EPSILON) * head_gain_ref[0:1, :]
            query = (query * cosine + swap_halves(query) * sine) * QUERY_UNIT
            out_ref[start, 0:128] = jnp.where(lane < HD, query, 0.0).astype(BF)
            if heads > 1:
                shifted = pltpu.roll(query, HD, 1)
                out_ref[start, 128:256] = jnp.where(lane < HD, shifted, 0.0).astype(BF)
            key = pair * lax.rsqrt(head_mean(pair * pair) + EPSILON) * head_gain_ref[1:2, :]
            key = key * cosine + swap_halves(key) * sine
            out_ref[start, 128 * heads : 128 * heads + 128] = jnp.where(lane < HD, key, pair).astype(BF)


def project_back_body(count, outs, dims, at_ref, *refs):
    x_refs = refs[:count]
    w_ref, rows_ref, mixing_ref, cos_ref, sin_ref, mine_ref, theirs_ref, head_gain_ref = refs[
        count : count + 8
    ]
    part_refs = refs[count + 8 : count + 8 + outs]
    dw_ref, acc_ref = refs[count + 8 + outs :]
    core = at_ref[count]
    gain = rows_ref[0:1, :]
    gain_sums = [jnp.zeros((1, 128), F32), jnp.zeros((1, 128), F32)]
    done = 0
    for k, low, size in tiles_of(x_refs):
        start = pl.ds(pl.multiple_of(at_ref[k] + low, 128), size)
        normed = (unit_norm(x_refs[k][low : low + size, :].astype(F32)) * gain).astype(BF)
        cosine, sine = cos_ref[start, :], sin_ref[start, :]
        lane = lax.broadcasted_iota(jnp.int32, cosine.shape, 1)
        part = None
        for u, (unit, grad_ref) in enumerate(((core, mine_ref), (1 - core, theirs_ref))):
            cols = pl.ds(pl.multiple_of(256 * unit, 256), 256)
            weight = w_ref[:, cols]
            raw_both = dot(normed, weight)
            pieces = []
            for kind in range(2):
                raw = raw_both[:, 128 * kind : 128 * kind + 128]
                upstream = grad_ref[start, 128 * kind : 128 * kind + 128].astype(F32)
                turned = upstream * cosine - swap_halves(upstream) * sine
                scale = lax.rsqrt(head_mean(raw * raw) + EPSILON)
                one = raw * scale
                gain_sums[kind] += jnp.sum(turned * one, axis=0, keepdims=True)
                turned = turned * head_gain_ref[kind : kind + 1, :]
                grad = scale * (turned - one * head_mean(turned * one))
                if kind == 1:
                    grad = jnp.where(lane < HD, grad, upstream)
                pieces.append(grad.astype(BF))
            grads = jnp.concatenate(pieces, axis=1)
            term = dot(grads, weight, NT)
            part = term if part is None else part + term
            update = dot(normed, grads, TN)
            acc_ref[u] = update if done == 0 else acc_ref[u] + update
        scatter_rows(part_refs, done, part.astype(BF))
        done += size
    highs = [g.astype(BF) for g in gain_sums]
    lows = [(g - x.astype(F32)).astype(BF) for g, x in zip(gain_sums, highs, strict=True)]
    gain_row = jnp.concatenate(highs + lows, axis=1)
    gain_rows = jnp.concatenate([gain_row, jnp.zeros((7, 512), BF)], axis=0)
    blocks, heads, rows = dims
    for u, unit in enumerate((core, 1 - core)):
        cols = pl.ds(pl.multiple_of(256 * unit, 256), 256)
        for h in range(heads):
            for b in range(blocks):
                low = (h * blocks + b) * rows
                at = h * (rows + 8)
                dw_ref[b, at : at + rows, cols] = acc_ref[u, low : low + rows, :].astype(BF)
                dw_ref[b, at + rows : at + rows + 8, :] = gain_rows
    for b in range(blocks):
        for i in range(mixing_ref.shape[1] // 512):
            at = heads * (rows + 8) + i * rows
            dw_ref[b, at : at + rows, :] = mixing_ref[
                b * rows : (b + 1) * rows, 512 * i : 512 * (i + 1)
            ]


def mix_body(places, at_ref, a_ref, *refs):
    m_refs = refs[: len(places)]
    own_ref, rows_ref, hidden_ref, normed_ref = refs[len(places) :]
    hidden = own_ref[...].astype(F32)
    cols = a_ref.shape[2]
    for (other, shift), m_ref in zip(places, m_refs, strict=True):
        if other is None:
            for h in range(a_ref.shape[0]):
                hidden += dot(a_ref[h], m_ref[h * cols : (h + 1) * cols, :])
        else:
            rows = m_ref.shape[0]
            hidden += dot(a_ref[at_ref[0] ^ other, :, shift : shift + rows], m_ref[...])
    hidden_ref[...] = hidden
    normed_ref[...] = (unit_norm(hidden) * rows_ref[1:2, :]).astype(BF)


def add_parts(addends, refs, rows, depth):
    half = rows // 2
    sums = [jnp.zeros((half, depth), F32), jnp.zeros((half, depth), F32)]
    for low, ref in zip(addends, refs, strict=True):
        whole = len(refs) == 1 or ref is refs[0]
        for i in range(2):
            if whole:
                sums[i] += ref[i * half : (i + 1) * half, :].astype(F32)
            elif low == i * half:
                sums[i] += ref[0:half, :].astype(F32)
    return jnp.concatenate(sums, axis=0)


def hidden_back_body(places, addends, at_ref, hidden_ref, cot_ref, rows_ref, *refs):
    m_refs = refs[: len(places)]
    add_refs = refs[len(places) : len(places) + len(addends)]
    grad_ref, low_ref, mixture_ref = refs[len(places) + len(addends) :]
    hidden = hidden_ref[...]
    upstream = add_parts(addends, add_refs, *hidden.shape) * rows_ref[1:2, :]
    scale = lax.rsqrt(jnp.mean(hidden * hidden, axis=1, keepdims=True) + EPSILON)
    one = hidden * scale
    grad = cot_ref[...].astype(F32) + scale * (
        upstream - one * jnp.mean(upstream * one, axis=1, keepdims=True)
    )
    grad_ref[...] = grad
    low = grad.astype(BF)
    low_ref[...] = low
    cols = mixture_ref.shape[2]
    for (other, shift), m_ref in zip(places, m_refs, strict=True):
        if other is None:
            for h in range(mixture_ref.shape[0]):
                mixture_ref[h] = dot(low, m_ref[h * cols : (h + 1) * cols, :], NT).astype(BF)
        else:
            rows = m_ref.shape[0]
            mixture_ref[at_ref[0] ^ other, :, shift : shift + rows] = dot(
                low, m_ref[...], NT
            ).astype(BF)


def input_back_body(addends, own_ref, grad_ref, rows_ref, *refs):
    out_ref = refs[-1]
    own = own_ref[...].astype(F32)
    upstream = add_parts(addends, refs[:-1], *own.shape) * rows_ref[0:1, :]
    scale = lax.rsqrt(jnp.mean(own * own, axis=1, keepdims=True) + EPSILON)
    one = own * scale
    grad = grad_ref[...] + scale * (
        upstream - one * jnp.mean(upstream * one, axis=1, keepdims=True)
    )
    out_ref[...] = grad.astype(BF)


def finish_feed_body(heads, order_ref, part_ref, weight_ref, gate_ref, up_ref, dot_ref):
    width = part_ref.shape[2]
    total = jnp.zeros(dot_ref.shape, F32)
    for k in range(heads):
        start = order_ref[k] * (width // 2)
        for n in range(0, width, 128):
            value = part_ref[k, :, n : n + 128].astype(F32)
            total += value * weight_ref[order_ref[k], :, n : n + 128].astype(F32)
            out = gate_ref if n % 256 == 0 else up_ref
            out[:, pl.ds(pl.multiple_of(start + n // 256 * 128, 128), 128)] = value
    dot_ref[...] = jnp.broadcast_to(jnp.sum(total, axis=1, keepdims=True), total.shape)


def finish_projections_body(heads, unit_heads, order_ref, part_ref, weight_ref, *refs):
    q_ref, *kv_refs, dot_ref, gain_ref = refs
    rows = dot_ref.shape[0]
    total = jnp.zeros(dot_ref.shape, F32)
    gains = jnp.zeros((8, 512), F32)
    lane = lax.broadcasted_iota(jnp.int32, (rows, 128), 1)
    for k in range(heads):
        head = order_ref[k]
        value = part_ref[k, 0:rows, :].astype(F32)
        gains += part_ref[k, rows : rows + 8, :].astype(F32)
        product = value * weight_ref[head].astype(F32)
        for n in range(0, 512, 128):
            total += product[:, n : n + 128]
        spot = pl.ds(pl.multiple_of(head * 128, 128), 128)
        first, second = value[:, 128:256], value[:, 384:512]
        if unit_heads == 2:
            start = pl.multiple_of(head * 256, 256)
            q_ref[:, pl.ds(start, 128)] = value[:, 0:128]
            q_ref[:, pl.ds(start + 128, 128)] = value[:, 256:384]
            k_ref, v_ref = kv_refs
            k_ref[:, spot] = jnp.where(lane < HD, first, pltpu.roll(second, HD, 1))
            v_ref[:, spot] = jnp.where(lane < HD, pltpu.roll(first, HD, 1), second)
        else:
            q_ref[:, spot] = jnp.where(
                lane < HD, value[:, 0:128], pltpu.roll(value[:, 256:384], HD, 1)
            )
            kv_refs[0][:, spot] = first + second
    dot_ref[...] = jnp.broadcast_to(jnp.sum(total, axis=1, keepdims=True), total.shape)
    gain_ref[...] = gains[:, 0:256] + gains[:, 256:512]


def output_body(addends, hidden_ref, *refs):
    refs[-1][...] = (
        hidden_ref[...] + add_parts(addends, refs[:-1], *hidden_ref.shape)
    ).astype(BF)


def joined(refs, scratch):
    if len(refs) == 1:
        return refs[0]
    at = 0
    for ref in refs:
        scratch[at : at + ref.shape[0], :] = ref[...]
        at += ref.shape[0]
    return scratch


def column_tiles(width, size=512):
    return [(n, min(size, width - n)) for n in range(0, width, size)]


def activation_grad_body(count, order_ref, *refs):
    c_refs, down_ref, out_refs, scratch = refs[:count], refs[count], refs[count + 1 : -1], refs[-1]
    cot = joined(c_refs, scratch)
    for n, size in column_tiles(down_ref.shape[0]):
        grad = dot(cot[...], down_ref[n : n + size, :], NT).astype(BF)
        at = 0
        for out in out_refs:
            out[:, n : n + size] = grad[at : at + out.shape[0]]
            at += out.shape[0]


def feed_forward_body(count, first, outs, place_ref, *refs):
    x_refs, grad_ref, weight_ref = refs[:count], refs[count], refs[count + 1]
    act_ref, out_ref = refs[count + 2 : count + 4]
    back_refs, scratch = refs[count + 4 : count + 4 + outs], refs[-3]
    gu_ref, sems = refs[-2:]
    heads, blocks, piece, width = gu_ref.shape
    depth = heads * blocks * piece
    copies = [
        pltpu.make_async_copy(weight_ref.at[:, h], gu_ref.at[place_ref[h]], sems.at[h])
        for h in range(heads)
    ]
    for copy in copies:
        copy.start()
    x = joined(x_refs, scratch)
    for copy in copies:
        copy.wait()
    for n, size in column_tiles(width):
        both = dot(x[...], gu_ref[:, :, :, n : n + size].reshape(depth, size))
        for m in range(0, size, 256):
            gate, up = both[:, m : m + 128], both[:, m + 128 : m + 256]
            cols = slice((n + m) // 2, (n + m) // 2 + 128)
            grad = grad_ref[:, cols].astype(F32)
            sig = jax.nn.sigmoid(gate)
            swish = gate * sig
            act_ref[:, cols] = (swish * up).astype(BF)
            out_ref[:, n + m : n + m + 128] = (
                grad * up * sig * (1.0 + gate * (1.0 - sig))
            ).astype(BF)
            out_ref[:, n + m + 128 : n + m + 256] = (grad * swish).astype(BF)
    for n, size in column_tiles(depth):
        group = size * heads // depth if size * heads >= depth else 0
        if group:
            first_head = n * heads // depth
            weight = gu_ref[first_head : first_head + group].reshape(size, width)
        back = dot(out_ref[...], weight, NT).astype(BF)
        cols = slice(n, n + size)
        if first is None:
            scatter_rows(back_refs, 0, back, cols)
        elif first:
            back_refs[0][:, cols] = back
        else:
            scatter_rows([None, *back_refs], x.shape[0] // 3, back, cols)


def feed_forward(xs, grad, gate_up, first):
    blocks, heads, piece, width = gate_up.shape
    depth = heads * blocks * piece
    rows = grad.shape[0]
    place = lax.axis_index("head")
    if first is None:
        outs = [shape(rows, depth)]
    elif first:
        outs = [shape(rows, depth)]
    else:
        outs = part_outs(rows // 3, depth)[1:]
    res = run(
        functools.partial(feed_forward_body, len(xs), first, len(outs)),
        [shape(rows, width // 2), shape(rows, width)] + outs,
        list(xs) + [grad, gate_up],
        flops=4 * rows * depth * width,
        exps=rows * width // 2,
        scalars=[place ^ k for k in range(heads)],
        scratch=[
            pltpu.VMEM((rows, depth), BF),
            pltpu.VMEM((heads, blocks, piece, width), BF),
            pltpu.SemaphoreType.DMA((heads,)),
        ],
        limit=48,
        stay=(len(xs) + 1,),
    )
    return res[0], res[1], res[2:]


def down_body(count, outs, *refs):
    a_refs, down_ref, out_refs, scratch = refs[:count], refs[count], refs[count + 1 : -1], refs[-1]
    act = joined(a_refs, scratch)
    for n, size in column_tiles(down_ref.shape[1]):
        scatter_rows(
            out_refs,
            0,
            dot(act[...], down_ref[:, n : n + size]).astype(BF),
            slice(n, n + size),
        )


def packed_rows(blocks, heads, piece, cols, width):
    chunks = cols // 1024
    rest = cols - 1024 * chunks
    aside = 1024 // rest if rest else heads
    tail = -(-heads // aside) * piece if rest else 0
    return chunks, rest, aside, chunks * heads * piece + tail, width // blocks


def weight_grad_body(counts, dims, packed, *refs):
    refs = list(refs)
    x_refs, c_refs, g_refs, a_refs = ([refs.pop(0) for _ in range(n)] for n in counts)
    out_ref, down_ref, x_all, c_all = (refs[0], refs[3], *refs[1:3]) if packed else refs
    blocks, heads, piece, cols, width = dims
    chunks, rest, aside, start, share = packed_rows(blocks, heads, piece, cols, width)

    def product(left, right, tile):
        total, at = None, 0
        for ref in right:
            here = slice(at, at + ref.shape[0])
            term = dot(left[here, :], ref[:, tile], TN)
            total = term if total is None else total + term
            at += ref.shape[0]
        return total.astype(BF)

    x = joined(x_refs, x_all)
    for n, size in column_tiles(cols):
        total = product(x, g_refs, slice(n, n + size))
        for h in range(heads):
            for b in range(blocks):
                low = (h * blocks + b) * piece
                value = total[low : low + piece]
                if n < 1024 * chunks:
                    row = n // 1024 * heads * piece + h * piece
                    out_ref[b, row : row + piece, n % 1024 : n % 1024 + size] = value
                else:
                    row = chunks * heads * piece + h // aside * piece
                    col = h % aside * rest
                    out_ref[b, row : row + piece, col : col + rest] = value
    cot = joined(c_refs, c_all)
    for n, size in column_tiles(down_ref.shape[0], 256):
        total, at = None, 0
        for ref in a_refs:
            here = slice(at, at + ref.shape[0])
            term = dot(ref[:, n : n + size], cot[here, :], TN)
            total = term if total is None else total + term
            at += ref.shape[0]
        down_ref[n : n + size, :] = total.astype(BF)
    if packed:
        for b in range(blocks):
            out_ref[b, start : start + share, :] = down_ref[b * share : (b + 1) * share, :]


def mixing_grad_body(count, at_ref, m_ref, *refs):
    total = None
    for k, low, size in tiles_of(refs[:count]):
        start = pl.ds(pl.multiple_of(at_ref[k] + low, 128), size)
        term = dot(m_ref[start, :], refs[k][low : low + size, :], TN)
        total = term if total is None else total + term
    refs[count][...] = total.astype(BF)


def permute(x, axis, move):
    count = lax.axis_size(axis)
    return lax.ppermute(x, axis, [(i, move(i) % count) for i in range(count)])


def together(*arrays):
    return lax.optimization_barrier(arrays)


def gather_near(x):
    if lax.axis_size("head") != 4:
        return []
    return [permute(x, "head", lambda i: i ^ 1), permute(x, "head", lambda i: i ^ 2)]


def gather_far(x, near):
    if lax.axis_size("head") != 4:
        return [lax.all_gather(x, "head", axis=0, tiled=True)]
    half = x.shape[0] // 2
    return [
        permute(near[0][:half], "head", lambda i: i ^ 2),
        permute(near[1][half:], "head", lambda i: i ^ 1),
    ]


def gathered(x, near, far):
    return [x, *near, *far] if near else list(far)


def part_places(rows):
    if lax.axis_size("head") != 4:
        return [(None, 0)]
    return [(0, 0), (1, 0), (2, 0), (3, 0), (3, rows // 2)]


def part_outs(rows, depth):
    if lax.axis_size("head") != 4:
        return [shape(rows * lax.axis_size("head"), depth)]
    half = rows // 2
    return [shape(rows, depth), shape(rows, depth), shape(rows, depth), shape(half, depth), shape(half, depth)]


def scatter_rows(refs, at, value, cols=None):
    cols = slice(None) if cols is None else cols
    if len(refs) == 1:
        refs[0][at : at + value.shape[0], cols] = value
        return
    own, by_one, by_two, stay_up, stay_low = refs
    half = stay_up.shape[0]
    spots = [
        (own, 0), (own, half), (by_one, 0), (stay_low, 0), (stay_up, 0), (by_two, 0), (by_one, half), (by_two, half)
    ]
    for i in range(value.shape[0] // half):
        ref, low = spots[at // half + i]
        ref[low : low + half, cols] = value[i * half : (i + 1) * half]


def sum_near(pieces):
    if len(pieces) == 1:
        return []
    return [
        permute(pieces[1], "head", lambda i: i ^ 1),
        permute(pieces[2], "head", lambda i: i ^ 2),
    ]


def sum_far(pieces, near):
    if len(pieces) == 1:
        return [lax.psum_scatter(pieces[0], "head", scatter_dimension=0, tiled=True)]
    stay_up, stay_low = pieces[3:]
    half = stay_up.shape[0]
    upper = (near[0][half:].astype(F32) + stay_up.astype(F32)).astype(BF)
    lower = (near[1][half:].astype(F32) + stay_low.astype(F32)).astype(BF)
    return [permute(upper, "head", lambda i: i ^ 2), permute(lower, "head", lambda i: i ^ 1)]


def sum_terms(pieces, near, far):
    if len(pieces) == 1:
        return [0], list(far)
    half = pieces[3].shape[0]
    return [0, 0, half, 0, half], [pieces[0], *near, *far]


def mirror(x):
    count = lax.axis_size("blk")
    return permute(x, "blk", lambda i: count - i if i % 2 else i)


def exchange_head(x):
    count = lax.axis_size("head")
    place = lax.axis_index("head")
    return jnp.stack(
        [
            permute(
                lax.dynamic_index_in_dim(x, place ^ k, 0, keepdims=False),
                "head",
                lambda i, k=k: i ^ k,
            )
            if k
            else lax.dynamic_index_in_dim(x, place, 0, keepdims=False)
            for k in range(count)
        ]
    )


def other_core(x):
    return permute(x, "blk", lambda i: i ^ 1)


def per_device(
    inputs,
    query_weight,
    key_weight,
    value_weight,
    mixing_weight,
    gate_weight,
    up_weight,
    down_weight,
    attention_gain,
    feedforward_gain,
    query_gain,
    key_gain,
    cotangent,
):
    heads = lax.axis_size("head")
    blocks = lax.axis_size("blk")
    chips = blocks // 2
    place = lax.axis_index("head")
    block = lax.axis_index("blk")
    core = block % 2
    chip = block // 2
    rows, depth = inputs.shape
    span = rows * heads
    piece = query_weight.shape[0]
    width = gate_weight.shape[1] // heads
    wide = -(-width // 128) * 128
    shared = KV // heads
    unit_heads = HQ // heads // 2
    unit_cols = unit_heads * HD

    qkv_own = jnp.concatenate(
        [
            jnp.pad(
                query_weight.reshape(piece, heads, 2, unit_cols),
                ((0, 0), (0, 0), (0, 0), (0, 128 - unit_cols)),
            ),
            jnp.repeat(key_weight.reshape(piece, heads, shared, HD), 2 // shared, axis=2),
            jnp.repeat(value_weight.reshape(piece, heads, shared, HD), 2 // shared, axis=2),
        ],
        axis=-1,
    ).reshape(piece, heads, 512)
    gains = jnp.pad(jnp.stack([attention_gain, feedforward_gain], axis=1), ((0, 0), (0, 126)))
    qkv_send = jnp.concatenate(
        [qkv_own, jnp.broadcast_to(gains[:, None, :], (piece, heads, 128))], axis=-1
    ).transpose(1, 0, 2)
    gate_up_send = (
        jnp.stack(
            [
                jnp.pad(
                    w.reshape(piece, heads, width), ((0, 0), (0, 0), (0, wide - width))
                ).reshape(piece, heads, wide // 128, 128)
                for w in (gate_weight, up_weight)
            ],
            axis=3,
        )
        .reshape(piece, heads, 2 * wide)
        .transpose(1, 0, 2)
    )

    own, qkv_piece = together(mirror(inputs), exchange_head(qkv_send))
    qkv_mine = [
        permute(qkv_piece, "blk", lambda i, step=step: i + 2 * step) for step in range(1, chips)
    ]
    qkv_mine, near, own, cotangent = together(qkv_mine, gather_near(own), own, cotangent)
    own_cot = mirror(cotangent)
    qkv_mine = jnp.stack([qkv_piece, *qkv_mine])
    low_rows, qkv_mine = together(
        jnp.concatenate([mixing_weight, down_weight], axis=0), qkv_mine
    )
    low_rows = lax.all_gather(low_rows, "blk", axis=0)
    qkv_theirs, far = together(other_core(qkv_mine), gather_far(own, near))
    xs = gathered(own, near, far)
    sources = [(chip - r) % chips for r in range(chips)]
    qkv_ext = run(
        functools.partial(assemble_body, heads),
        shape(heads, blocks, piece, 640),
        [qkv_mine, qkv_theirs],
        scalars=[2 * z + core for z in sources]
        + [2 * z + 1 - core for z in sources]
        + [place ^ k for k in range(heads)],
    ).reshape(depth, 640)
    span_index = jnp.where(core == 0, block, blocks - block)
    positions = (span_index * span + jnp.arange(span, dtype=jnp.int32)).astype(F32)
    lane = jnp.arange(128, dtype=jnp.int32)
    frequency = jnp.exp(
        (lane % (HD // 2)).astype(F32) * (-2.0 * math.log(ROPE_BASE) / HD)
    )
    angles = positions[:, None] * frequency[None, :]
    cosine = jnp.cos(angles)
    sine = jnp.sin(angles) * jnp.where(lane % HD < HD // 2, -1.0, 1.0)
    head_gain = jnp.concatenate(
        [
            jnp.tile(query_gain.astype(F32), 2)[None, :],
            jnp.tile(key_gain.astype(F32), 2)[None, :],
            jnp.zeros((6, 128), F32),
        ],
        axis=0,
    )

    places = part_places(rows)
    starts = [0 if other is None else (place ^ other) * rows + shift for other, shift in places]
    packet = 128 * (unit_heads + 1)
    keep, send, gain_rows = run(
        functools.partial(project_body, len(xs), unit_heads),
        [shape(span, packet), shape(span, packet), shape(8, depth, dtype=F32)],
        xs + [qkv_ext, cosine, sine, head_gain],
        flops=4 * span * depth * 512,
        scalars=starts + [core],
        far=tuple(range(len(xs) + 4)),
    )
    gate_up_send, keep = together(gate_up_send, keep)
    send, gate_up_piece = together(other_core(send), exchange_head(gate_up_send))
    packets = jnp.concatenate([keep, send], axis=0)
    kv = packets[:, -128:]

    def slot_of(early, z):
        return jnp.where(4 * z < blocks, early, 1 - early) ^ core ^ 1

    def reach(z):
        return jnp.abs(4 * z - (blocks - 1))

    my_low, my_high = slot_of(1, chip), slot_of(0, chip)

    def offsets(step):
        if step == 0:
            return [span * my_high, span * my_low]
        source = (chip - step) % chips
        low, high = slot_of(1, source), slot_of(0, source)
        outer = reach(source) > reach(chip)
        return [
            span * jnp.where(outer, my_low, my_high),
            span * low,
            span * my_high,
            span * jnp.where(outer, low, high),
        ]

    def next_chip(x):
        return permute(x, "blk", lambda i: i + 2)

    kvs = [kv]
    acc = None
    cot_near = cot_far = mixing_near = mixing_far = []
    mixing_rows, down_full = None, None
    for step in range(chips):
        last = step == chips - 1
        res = attend(offsets(step), packets, kvs[step], acc, step == 0, last, unit_heads)
        ahead = [] if last else [next_chip(kvs[step])]
        if step == min(1, chips - 1):
            cot_near = gather_near(own_cot)
        if step == min(2, chips - 1):
            mixing_rows = low_rows[:, :piece].reshape(blocks * piece, depth)
            down_full = jnp.pad(
                low_rows[:, piece:].reshape(-1, depth), ((0, wide - width), (0, 0))
            )
            mixing_near = gather_near(mixing_rows)
            cot_far = gather_far(own_cot, cot_near)
        if last:
            mixing_far = gather_far(mixing_rows, mixing_near)
        res, ahead, own_cot, cot_near, cot_far, mixing_near, mixing_far = together(
            res, ahead, own_cot, cot_near, cot_far, mixing_near, mixing_far
        )
        acc = res[0]
        kvs += ahead
        if step == min(1, chips - 1):
            acc, gate_up_piece = together(acc, gate_up_piece)
            gate_up = lax.all_gather(gate_up_piece, "blk", axis=0)
    cots = gathered(own_cot, cot_near, cot_far)
    mixing_parts = gathered(mixing_rows, mixing_near, mixing_far)
    mixture_pair = res[1][:, :, :unit_cols]
    theirs = other_core(mixture_pair[1])
    mixture_span = jnp.where(
        core == 0,
        jnp.concatenate([mixture_pair[0], theirs], axis=1),
        jnp.concatenate([theirs, mixture_pair[0]], axis=1),
    )
    mixture = lax.all_to_all(
        mixture_span.reshape(heads, rows, 2 * unit_cols), "head", 0, 0, tiled=True
    )
    mix_places = part_places(mixing_rows.shape[0])
    hidden, normed_ffn = run(
        functools.partial(mix_body, mix_places),
        [shape(rows, depth, dtype=F32), shape(rows, depth)],
        [mixture] + mixing_parts + [own, gain_rows],
        flops=2 * rows * depth * depth,
        scalars=[place],
        far=tuple(range(1, len(mixing_parts) + 3)),
    )
    split = heads == 4
    grads = run(
        functools.partial(activation_grad_body, len(cots)),
        [shape(rows, wide), shape(span - rows, wide)] if split else [shape(span, wide)],
        [normed_ffn] + cots + [down_full],
        flops=2 * span * depth * wide,
        scratch=[pltpu.VMEM((span, depth), BF)],
        far=tuple(range(1, len(cots) + 2)),
        stay=(0,),
    )
    near, grads, normed_ffn = together(gather_near(normed_ffn), grads, normed_ffn)
    far = gather_far(normed_ffn, near)
    results = []
    if split:
        results.append(feed_forward([normed_ffn], grads[0], gate_up, True))
    far, results = together(far, results)
    ffn_parts = gathered(normed_ffn, near, far)
    if split:
        results = [*results, feed_forward(ffn_parts[1:], grads[1], gate_up, False)]
    else:
        results = [feed_forward(ffn_parts, grads[0], gate_up, None)]
    acts = [r[0] for r in results]
    gate_up_grads = [r[1] for r in results]
    backs = [b for r in results for b in r[2]]
    counts = (len(ffn_parts), len(cots), len(gate_up_grads), len(acts))
    dims = (blocks, heads, piece, 2 * wide, width)
    chunks, rest_cols, aside, start_row, share = packed_rows(*dims)
    packed = share % 16 == 0 and start_row % 16 == 0
    ffn_rows = start_row + (share if packed else 0)
    res = run(
        functools.partial(weight_grad_body, counts, dims, packed),
        [shape(blocks, ffn_rows, 1024)] + ([] if packed else [shape(wide, depth)]),
        ffn_parts + cots + gate_up_grads + acts,
        flops=6 * span * depth * wide,
        scratch=[pltpu.VMEM((span, depth), BF)] * 2
        + ([pltpu.VMEM((wide, depth), BF)] if packed else []),
        limit=56,
        far=tuple(range(len(ffn_parts) + len(cots))),
    )
    near, res, backs = together(sum_near(backs), list(res) if not packed else list(res)[:1], backs)
    ffn_part = lax.psum_scatter(res[0], "blk", scatter_dimension=0, tiled=True)[0]
    far = sum_far(backs, near)
    down_full, near = together(down_full, near)
    terms = run(
        functools.partial(down_body, len(acts), len(part_outs(rows, depth))),
        part_outs(rows, depth),
        acts + [down_full],
        flops=2 * span * depth * wide,
        scratch=[pltpu.VMEM((span, wide), BF)],
    )
    far, terms = together(far, terms)
    shifts, addends = sum_terms(backs, near, far)
    hidden_grad, hidden_low, mixture_grad = run(
        functools.partial(hidden_back_body, mix_places, shifts),
        [shape(rows, depth, dtype=F32), shape(rows, depth), shape(heads, rows, 2 * unit_cols)],
        [hidden, own_cot, gain_rows] + mixing_parts + addends,
        flops=2 * rows * depth * depth,
        scalars=[place],
        far=tuple(range(len(mixing_parts) + 3)),
    )
    grad_span = lax.all_to_all(mixture_grad, "head", 0, 0, tiled=True).reshape(span, 2 * unit_cols)
    theirs = other_core(
        jnp.where(core == 0, grad_span[:, unit_cols:], grad_span[:, :unit_cols])
    )
    if unit_cols < 128:
        pad = ((0, 0), (0, 128 - unit_cols))
        theirs = jnp.pad(theirs, pad)
        grad_wide = jnp.concatenate(
            [jnp.pad(grad_span[:, :unit_cols], pad), jnp.pad(grad_span[:, unit_cols:], pad)], axis=1
        )
    else:
        grad_wide = grad_span
    out_grad = run(
        out_grad_body,
        shape(unit_heads, 2 * span, 128),
        [grad_wide, theirs, acc],
        scalars=[core],
    )

    def columns_of(ffn_part):
        part = ffn_part[:start_row]
        pieces = [
            part[i * heads * piece : (i + 1) * heads * piece].reshape(heads, piece, 1024)
            for i in range(chunks)
        ]
        if rest_cols:
            part = part[chunks * heads * piece :].reshape(-1, piece, aside, rest_cols)
            pieces.append(part.transpose(0, 2, 1, 3).reshape(heads, piece, rest_cols))
        return jnp.concatenate(pieces, axis=-1)

    query_acc = None
    sent, arrived = [], []
    hidden_near = hidden_far = term_near = term_far = []
    steps = sorted(range(1, chips), key=lambda step: min(step, chips - step)) + [0]
    for at, step in enumerate(steps):
        last = at == len(steps) - 1
        query_acc, kv_grad = attend_back(
            offsets(step), packets, out_grad, kvs[step], query_acc, step == 0
        )
        moved = [
            permute(g, "blk", lambda i, back=back: i - 2 * back) for back, g in sent
        ]
        if at == 0:
            hidden_near = gather_near(hidden_low)
        if at == min(1, chips - 1):
            hidden_far = gather_far(hidden_low, hidden_near)
        if at == min(1, chips - 1):
            term_near = sum_near(terms)
        if at == min(2, chips - 1):
            term_far = sum_far(terms, term_near)
            hidden_parts = gathered(hidden_low, hidden_near, hidden_far)
            mixing_grad = run(
                functools.partial(mixing_grad_body, len(hidden_parts)),
                shape(2 * unit_cols, depth),
                [mixture_span] + hidden_parts,
                flops=4 * span * depth * unit_cols,
                scalars=starts,
                far=tuple(range(len(hidden_parts) + 1)),
            )
        if last:
            gate_up_part = exchange_head(gate_up_part)
        query_acc, kv_grad, hidden_near, hidden_far, terms, term_near, term_far = together(
            query_acc, kv_grad, hidden_near, hidden_far, terms, term_near, term_far
        )
        if at == max(len(steps) - 2, 0):
            query_acc, ffn_part, mixing_grad = together(query_acc, ffn_part, mixing_grad)
            gate_up_part = columns_of(ffn_part)
        arrived += moved
        sent = [(step, kv_grad)] if step else []
    if packed:
        down_sum = ffn_part[start_row:]
    else:
        down_sum = lax.psum_scatter(res[1][:width], "blk", scatter_dimension=0, tiled=True)
    mine, theirs = run(
        pack_body,
        [shape(span, 256), shape(span, 256)],
        [query_acc, kv_grad] + arrived,
    )
    theirs, mine, hidden = together(other_core(theirs), mine, hidden)
    back = run(
        functools.partial(
            project_back_body, len(xs), len(part_outs(rows, depth)), (blocks, heads, piece)
        ),
        part_outs(rows, depth)
        + [shape(blocks, heads * (piece + 8) + depth // 512 * piece, 512)],
        xs + [qkv_ext, gain_rows, mixing_grad, cosine, sine, mine, theirs, head_gain],
        flops=12 * span * depth * 512,
        scalars=starts + [core],
        scratch=[pltpu.VMEM((2, depth, 256), F32)],
        far=tuple(range(len(xs) + 6)),
    )
    *back, projections = back
    projections = lax.psum_scatter(projections, "blk", scatter_dimension=0, tiled=True)[0]
    output_shifts, output_terms = sum_terms(terms, term_near, term_far)
    gate_up_part, back, hidden = together(gate_up_part, back, hidden)
    near = sum_near(back)
    output = run(
        functools.partial(output_body, output_shifts),
        shape(rows, depth),
        [hidden] + output_terms,
        far=(0, 1),
    )
    gate_sum, up_sum, feed_gain_sum = run(
        functools.partial(finish_feed_body, heads),
        [shape(piece, heads * wide, dtype=F32)] * 2 + [shape(piece, 128, dtype=F32)],
        [gate_up_part, gate_up_send],
        scalars=[place ^ k for k in range(heads)],
    )
    near, output, gate_sum, up_sum, feed_gain_sum, down_sum = together(
        near, output, gate_sum, up_sum, feed_gain_sum, down_sum.astype(F32)
    )
    output = mirror(output)
    far = sum_far(back, near)
    input_shifts, addends = sum_terms(back, near, far)
    input_gradient = run(
        functools.partial(input_back_body, input_shifts),
        shape(rows, depth),
        [own, hidden_grad, gain_rows] + addends,
    )
    input_gradient = mirror(input_gradient)
    cut = heads * (piece + 8)
    mixing_sum = (
        projections[cut:].reshape(depth // 512, piece, 512).transpose(1, 0, 2).reshape(piece, depth)
    ).astype(F32)
    qkv_part = exchange_head(projections[:cut].reshape(heads, piece + 8, 512))
    outs = [shape(piece, heads * 2 * unit_cols, dtype=F32)]
    outs += [shape(piece, heads * 128, dtype=F32)] * shared
    *grads, attention_gain_sum, head_gain_sum = run(
        functools.partial(finish_projections_body, heads, unit_heads),
        outs + [shape(piece, 128, dtype=F32), shape(8, 256, dtype=F32)],
        [qkv_part, qkv_own.transpose(1, 0, 2)],
        scalars=[place ^ k for k in range(heads)],
    )
    if shared == 1:
        both = grads[1].reshape(piece, heads, 2, HD)
        grads = [grads[0], both[:, :, 0].reshape(piece, -1), both[:, :, 1].reshape(piece, -1)]

    def only(x):
        return x.reshape(piece, heads, wide)[..., :width].reshape(piece, -1)

    return (
        output,
        input_gradient,
        *grads,
        mixing_sum,
        only(gate_sum),
        only(up_sum),
        down_sum,
        attention_gain_sum[:, 0] / attention_gain.astype(F32),
        feed_gain_sum[:, 0] / feedforward_gain.astype(F32),
        head_gain_sum[0, :HD] + head_gain_sum[0, HD : 2 * HD],
        head_gain_sum[0, 128 : 128 + HD],
    )


def solution(mesh):
    in_specs = (
        P(("blk", "head"), None),
        P(("head", "blk"), None),
        P(("head", "blk"), None),
        P(("head", "blk"), None),
        P(("head", "blk"), None),
        P(("head", "blk"), None),
        P(("head", "blk"), None),
        P(("head", "blk"), None),
        P(("head", "blk")),
        P(("head", "blk")),
        P(),
        P(),
        P(("blk", "head"), None),
    )
    out_specs = (
        P(("blk", "head"), None),
        P(("blk", "head"), None),
        P(("head", "blk"), None),
        P(("head", "blk"), None),
        P(("head", "blk"), None),
        P(("head", "blk"), None),
        P(("head", "blk"), None),
        P(("head", "blk"), None),
        P(("head", "blk"), None),
        P(("head", "blk")),
        P(("head", "blk")),
        P(),
        P(),
    )
    return jax.shard_map(
        per_device, mesh=mesh, in_specs=in_specs, out_specs=out_specs, check_vma=False
    )
```

time: 667 us -> 460 us (0.69)
  waiting for transfers between devices: 251 us -> 70.5 us
  Pallas kernels: 97.1 us -> 218 us
  local copies, waits for them, and re-layouts: 85.3 us -> 33.6 us
  matrix products: 46.5 us -> 0 us
  other arithmetic: 54.5 us -> 17.2 us
  starting transfers between devices: 96.8 us -> 85.6 us
    pallas_call x10 -> x25, Pallas kernels: 97.1 us -> 218 us  [run(): pl.pallas_call(body, out_shape=tuple(outs) if many else outs[0], in_specs...]
    ppermute x51 -> x62, waiting for transfers between devices: 185 us -> 67.7 us  [permute(): return lax.ppermute(x, axis, [(i, move(i) % count) for i in range(count)])]
    reduce_scatter x4 -> x2, waiting for transfers between devices: 52.5 us -> 0.02 us  [the longest x1 0.02 us: per_device(): lax.psum_scatter(res[0], 'blk', scatter_dimension=0, tiled=True)[0]]
    dot_general x10 -> x0, matrix products: 46.5 us -> none  [dot(): return lax.dot_general(a, b, dims, preferred_element_type=F32)]
    dynamic_update_slice x23 -> x0, local copies, waits for them, and re-layouts: 21.4 us -> none  [gather_head(): lax.dynamic_update_slice(out, part, ((place ^ other) * rows + shift, 0))]
    convert_element_type x22 -> x7, other arithmetic: 21.5 us -> 1.27 us  [the longest x1 0.87 us: per_device(): down_sum.astype(F32)]
    all_to_all x5 -> x1, starting transfers between devices: 18.7 us -> 3.49 us  [per_device(): lax.all_to_all(mixture_grad, 'head', 0, 0, tiled=True)]
    all_to_all x5 -> x1, waiting for transfers between devices: 13.8 us -> 2.75 us  [per_device(): lax.all_to_all(mixture_grad, 'head', 0, 0, tiled=True)]
  transfers between devices with their start and end apart: 63 -> 67, of which waited for: 31 -> 30; matrix products, arithmetic and copies ran while one was open for 21% -> 8% of each run, Pallas kernels for 15% -> 41%
where the time goes in v2:
time: 460 us; the launch traced here: 451 us
  Pallas kernels  218 us (47%)
  starting transfers between devices  85.6 us (19%)
  waiting for transfers between devices  70.5 us (15%)
  local copies, waits for them, and re-layouts  33.6 us (7%)
  other arithmetic  17.2 us (4%)
  between operations  15.5 us (3%)
  blocking collectives  11 us (2%)
    pallas_call x25, Pallas kernels, run(): pl.pallas_call(body, out_shape=tuple(outs) if many else outs[0], in_specs...  218 us
    ppermute x62, starting transfers between devices, permute(): return lax.ppermute(x, axis, [(i, move(i) % count) for i in range(count)])  81.5 us
    ppermute x62, waiting for transfers between devices, permute(): return lax.ppermute(x, axis, [(i, move(i) % count) for i in range(count)])  67.7 us
    unnamed x130, local copies, waits for them, and re-layouts  11.6 us
    all_to_all x1, blocking collectives, per_device(): lax.all_to_all(mixture_span.reshape(heads, rows, 2 * unit_cols), 'head',...  11 us
  transfers between devices with their start and end apart: 67, of which 30 were waited for; matrix products, arithmetic and copies ran while one was open for 8% of the time, Pallas kernels for 41%

profile of v2, /device:TPU:9, one launch (start us, length us, event | category | flops | bytes accessed | tf_op | source)
XLA Modules:
  0.0 451.1 jit_solution(16474031570685834341)
XLA Ops:
  29.2 9.4 %collective-permute-done.6 = bf16[4,32,640]{2,1,0:T(8,128)(2,1)S(1)} collective-permute-done((bf16[4,32,640]{2,1,0:T(8,128)(2,1)S(1)}, bf16[4,32,640]{2,1,0:T(8,128)(2,1)S(1)}, u32[]{:S(2)}, u32[]{:S(2)}) %collective-permute-start.6) | collective-permute-done | bytes 163872 | tf_op jit(solution)/shard_map/ppermute | solution.py:723
  57.2 8.8 %shard_map.229 = (bf16[1024,384]{1,0:T(8,128)(2,1)}, bf16[1024,384]{1,0:T(8,128)(2,1)}, f32[8,1024]{1,0:T(8,128)}) custom-call(s32[6]{0:T(128)} %stack.257.refs_0_, bf16[256,1024]{1,0:T(8,128)(2,1)} %copy-done.1, bf16[256,1024]{1,0:T(8,128)(2,1)} %copy-done.14, bf16[256,1024]{1,0:T(8,128)(2,1)} %copy-done.13, bf16[128,1024]{1,0:T(8,128)(2,1)} %copy-done.32, ...), custom_call_target="tpu_custom_call" | custom-call | flops 1 | bytes 1 | tf_op jit(solution)/shard_map/pallas_call | solution.py:66
  82.7 9.5 %shard_map.230.refs_3_ = f32[2,2048,128]{2,1,0:T(8,128)} custom-call(s32[2]{0:T(128)} %pad_add_fusion.3.off_ref.refs_0_, bf16[2048,384]{1,0:T(8,128)(2,1)} %copy-done, bf16[2048,128]{1,0:T(8,128)(2,1)} %copy-done.6), custom_call_target="tpu_custom_call" | custom-call | flops 1 | bytes 1 | tf_op jit(solution)/shard_map/pallas_call | solution.py:66
  92.1 5.8 %collective-permute-done.17.refs_1_.refs_5_.refs_2_ = bf16[256,1024]{1,0:T(8,128)(2,1)S(1)} collective-permute-done((bf16[256,1024]{1,0:T(8,128)(2,1)}, bf16[256,1024]{1,0:T(8,128)(2,1)S(1)}, u32[]{:S(2)}, u32[]{:S(2)}) %collective-permute-start.17) | collective-permute-done | bytes 524320 | tf_op jit(solution)/shard_map/ppermute | solution.py:723
  101.5 9.2 %shard_map.231.refs_3_ = f32[2,2048,128]{2,1,0:T(8,128)} custom-call(s32[4]{0:T(128)} %pad_add_fusion.2.refs_0_, bf16[2048,384]{1,0:T(8,128)(2,1)} %copy-done, bf16[2048,128]{1,0:T(8,128)(2,1)} %collective-permute-done.16.refs_2_.refs_3_, f32[2,2048,128]{2,1,0:T(8,128)} %shard_map.230.refs_3_), custom_call_target="tpu_custom_call" | custom-call | flops 1 | bytes 1 | tf_op jit(solution)/shard_map/pallas_call | solution.py:66
  120.4 9.5 %shard_map.232.refs_3_ = f32[2,2048,128]{2,1,0:T(8,128)} custom-call(s32[4]{0:T(128)} %pad_add_fusion.refs_0_, bf16[2048,384]{1,0:T(8,128)(2,1)} %copy-done, bf16[2048,128]{1,0:T(8,128)(2,1)} %copy-done.16, f32[2,2048,128]{2,1,0:T(8,128)} %shard_map.231.refs_3_), custom_call_target="tpu_custom_call" | custom-call | flops 1 | bytes 1 | tf_op jit(solution)/shard_map/pallas_call | solution.py:66
  136.9 9.4 %shard_map.233 = (f32[2,2048,128]{2,1,0:T(8,128)}, bf16[2,1024,128]{2,1,0:T(8,128)(2,1)}) custom-call(s32[4]{0:T(128)} %pad_add_fusion.1.refs_0_, bf16[2048,384]{1,0:T(8,128)(2,1)} %copy-done, bf16[2048,128]{1,0:T(8,128)(2,1)} %collective-permute-done.21.refs_2_.refs_3_, f32[2,2048,128]{2,1,0:T(8,128)} %shard_map.232.refs_3_), custom_call_target="tpu_custom_call" | custom-call | flops 1 | bytes 1 | tf_op jit(solution)/shard_map/pallas_call | solution.py:66
  150.6 11.0 %all_to_all.10.refs_1_ = bf16[4,256,256]{2,1,0:T(8,128)(2,1)} all-to-all(bf16[4,256,256]{2,1,0:T(8,128)(2,1)S(1)} %maximum_select_fusion), channel_id=1, replica_groups=mesh['head'=4,'blk'=8] {'head'}, dimensions={0} | all-to-all | bytes 1048576 | tf_op jit(solution)/shard_map/all_to_all | solution.py:1006
  171.1 6.6 %shard_map.235 = (bf16[256,1152]{1,0:T(8,128)(2,1)}, bf16[768,1152]{1,0:T(8,128)(2,1)}) custom-call(bf16[256,1024]{1,0:T(8,128)(2,1)} %get-tuple-element.248.refs_0_, bf16[256,1024]{1,0:T(8,128)(2,1)} %copy-done.3, bf16[256,1024]{1,0:T(8,128)(2,1)} %copy-done.8, bf16[256,1024]{1,0:T(8,128)(2,1)} %copy-done.7, ...), custom_call_target="tpu_custom_call" | custom-call | flops 1 | bytes 1 | tf_op jit(solution)/shard_map/pallas_call | solution.py:66
  181.9 7.1 %shard_map.236 = (bf16[256,1152]{1,0:T(8,128)(2,1)}, bf16[256,2304]{1,0:T(8,128)(2,1)}, bf16[256,1024]{1,0:T(8,128)(2,1)}) custom-call(s32[4]{0:T(128)} %pad_add_fusion.4.place_ref.order_ref, bf16[256,1024]{1,0:T(8,128)(2,1)} %get-tuple-element.248.refs_0_, bf16[256,1152]{1,0:T(8,128)(2,1)} %get-tuple-element.249.refs_1_, bf16[8,4,32,2304]{3,2,1,0:T(8,128)(2,1)} %bitcast.112), custom_call_target="tpu_custom_call" | custom-call | flops 1 | bytes 1 | tf_op jit(solution)/shard_map/pallas_call | solution.py:66
  189.9 13.1 %shard_map.237 = (bf16[768,1152]{1,0:T(8,128)(2,1)}, bf16[768,2304]{1,0:T(8,128)(2,1)}, bf16[256,1024]{1,0:T(8,128)(2,1)}, bf16[256,1024]{1,0:T(8,128)(2,1)}, bf...) custom-call(s32[4]{0:T(128)} %pad_add_fusion.4.place_ref.order_ref, bf16[256,1024]{1,0:T(8,128)(2,1)} %copy-done.10, ...), custom_call_target="tpu_custom_call" | custom-call | flops 1 | bytes 1 | tf_op jit(solution)/shard_map/pallas_call | solution.py:66
  204.5 16.0 %shard_map.238 = bf16[8,432,1024]{2,1,0:T(8,128)(2,1)} custom-call(bf16[256,1024]{1,0:T(8,128)(2,1)} %get-tuple-element.248.refs_0_, bf16[256,1024]{1,0:T(8,128)(2,1)} %copy-done.10, bf16[256,1024]{1,0:T(8,128)(2,1)} %copy-done.9, bf16[128,1024]{1,0:T(8,128)(2,1)} %copy-done.28, bf16[128,1024]{1,0:T(8,128)(2,1)} %copy-done.27, bf16[256,1024]{1,0:T(8,128)(2,1)} %copy-done.3, ...), custom_call_target="tpu_custom_call" | custom-call | flops 1 | bytes 1 | tf_op jit(solution)/shard_map/pallas_call | solution.py:66
  223.5 6.4 %shard_map.239 = (bf16[256,1024]{1,0:T(8,128)(2,1)}, bf16[256,1024]{1,0:T(8,128)(2,1)}, bf16[256,1024]{1,0:T(8,128)(2,1)}, bf16[128,1024]{1,0:T(8,128)(2,1)}, bf16[128,1024]{1,0:T(8,128)(2,1)}) custom-call(bf16[256,1152]{1,0:T(8,128)(2,1)} %get-tuple-element.261.refs_12_.refs_0_, bf16[768,1152]{1,0:T(8,128)(2,1)} %get-tuple-element.262.refs_13_.refs_1_, ...), custom_call_target="tpu_custom_call" | custom-call | flops 1 | bytes 1 | tf_op jit(solution)/shard_map/pallas_call | solution.py:66
  230.7 5.9 %shard_map.240 = (f32[256,1024]{1,0:T(8,128)}, bf16[256,1024]{1,0:T(8,128)(2,1)}, bf16[4,256,256]{2,1,0:T(8,128)(2,1)}) custom-call(s32[1]{0:T(128)} %bitcast.32.refs_0_, f32[256,1024]{1,0:T(8,128)} %get-tuple-element.342.refs_1_.refs_0_, bf16[256,1024]{1,0:T(8,128)(2,1)} %copy-done.3, f32[8,1024]{1,0:T(8,128)} %get-tuple-element.236.refs_8_.refs_3_.refs_7_.rows_ref, ...), custom_call_target="tpu_custom_call" | custom-call | flops 1 | bytes 1 | tf_op jit(solution)/shard_map/pallas_call | solution.py:66
  246.0 7.6 %collective-permute-start.37 = (bf16[1024,128]{1,0:T(8,128)(2,1)S(1)}, bf16[1024,128]{1,0:T(8,128)(2,1)S(1)}, u32[]{:S(2)}, u32[]{:S(2)}) collective-permute-start(bf16[1024,128]{1,0:T(8,128)(2,1)S(1)} %slice_select_fusion), channel_id=1, source_target_pairs={{0,1},{1,0},{2,3},{3,2},{4,5},{5,4},{6,7},{7,6},{8,9},{9,8},{10,11... | collective-permute-start | bytes 786440 | tf_op jit(solution)/shard_map/ppermute | solution.py:723
  255.4 5.0 %shard_map.241.refs_2_ = bf16[2,2048,128]{2,1,0:T(8,128)(2,1)} custom-call(s32[1]{0:T(128)} %bitcast.10.core_ref, bf16[1024,256]{1,0:T(8,128)(2,1)} %bitcast.119, bf16[1024,128]{1,0:T(8,128)(2,1)} %copy-done.53, f32[2,2048,128]{2,1,0:T(8,128)} %get-tuple-element.282.acc_ref), custom_call_target="tpu_custom_call" | custom-call | flops 1 | bytes 1 | tf_op jit(solution)/shard_map/pallas_call | solution.py:66
  260.4 16.0 %shard_map.242 = (f32[2,2048,128]{2,1,0:T(8,128)}, bf16[2048,128]{1,0:T(8,128)(2,1)}) custom-call(s32[4]{0:T(128)} %pad_add_fusion.2.refs_0_, bf16[2048,384]{1,0:T(8,128)(2,1)} %copy-done, bf16[2,2048,128]{2,1,0:T(8,128)(2,1)} %shard_map.241.refs_2_, bf16[2048,128]{1,0:T(8,128)(2,1)} %collective-permute-done.16.refs_2_.refs_3_), custom_call_target="tpu_custom_call" | custom-call | flops 1 | bytes 1 | tf_op jit(solution)/shard_map/pallas_call | solution.py:66
  279.6 17.0 %shard_map.243 = (f32[2,2048,128]{2,1,0:T(8,128)}, bf16[2048,128]{1,0:T(8,128)(2,1)}) custom-call(s32[4]{0:T(128)} %pad_add_fusion.1.refs_0_, bf16[2048,384]{1,0:T(8,128)(2,1)} %copy-done, bf16[2,2048,128]{2,1,0:T(8,128)(2,1)} %shard_map.241.refs_2_, bf16[2048,128]{1,0:T(8,128)(2,1)} %collective-permute-done.21.refs_2_.refs_3_, ...), custom_call_target="tpu_custom_call" | custom-call | flops 1 | bytes 1 | tf_op jit(solution)/shard_map/pallas_call | solution.py:66
  300.5 16.3 %shard_map.244 = (f32[2,2048,128]{2,1,0:T(8,128)}, bf16[2048,128]{1,0:T(8,128)(2,1)}) custom-call(s32[4]{0:T(128)} %pad_add_fusion.refs_0_, bf16[2048,384]{1,0:T(8,128)(2,1)} %copy-done, bf16[2,2048,128]{2,1,0:T(8,128)(2,1)} %shard_map.241.refs_2_, bf16[2048,128]{1,0:T(8,128)(2,1)} %copy-done.16, f32[2,2048,128]{2,1,0:T(8,128)} %get-tuple-element.301.refs_4_), custom_call_target="tpu_custom_call" | custom-call | flops 1 | bytes 1 | tf_op jit(solution)/shard_map/pallas_call | solution.py:66
  327.4 20.9 %shard_map.246 = (f32[2,2048,128]{2,1,0:T(8,128)}, f32[2048,128]{1,0:T(8,128)}) custom-call(s32[2]{0:T(128)} %pad_add_fusion.3.off_ref.refs_0_, bf16[2048,384]{1,0:T(8,128)(2,1)} %copy-done, bf16[2,2048,128]{2,1,0:T(8,128)(2,1)} %shard_map.241.refs_2_, bf16[2048,128]{1,0:T(8,128)(2,1)} %copy-done.6, f32[2,2048,128]{2,1,0:T(8,128)} %get-tuple-element.317.refs_4_), custom_call_target="tpu_custom_call" | custom-call | flops 1 | bytes 1 | tf_op jit(solution)/shard_map/pallas_call | solution.py:66
  359.2 14.4 %shard_map.248 = (bf16[256,1024]{1,0:T(8,128)(2,1)}, bf16[256,1024]{1,0:T(8,128)(2,1)}, bf16[256,1024]{1,0:T(8,128)(2,1)}, bf16[128,1024]{1,0:T(8,128)(2,1)}, bf...) custom-call(s32[6]{0:T(128)} %stack.257.refs_0_, bf16[256,1024]{1,0:T(8,128)(2,1)} %copy-done.1, ...), custom_call_target="tpu_custom_call" | custom-call | flops 1 | bytes 1 | tf_op jit(solution)/shard_map/pallas_call | solution.py:66
  402.2 5.5 %collective-permute-start.55 = (bf16[256,1024]{1,0:T(8,128)(2,1)}, bf16[256,1024]{1,0:T(8,128)(2,1)S(1)}, u32[]{:S(2)}, u32[]{:S(2)}) collective-permute-start(bf16[256,1024]{1,0:T(8,128)(2,1)} %shard_map.249), channel_id=1, source_target_pairs={{0,0},{1,7},{2,2},{3,5},{4,4},{5,3},{6,6},{7,1},{8,8},{9,15},{10,1... | collective-permute-start | bytes 1572872 | tf_op jit(solution)/shard_map/ppermute | solution.py:723
  412.0 5.1 %collective-permute-start.58 = (bf16[256,1024]{1,0:T(8,128)(2,1)}, bf16[256,1024]{1,0:T(8,128)(2,1)S(1)}, u32[]{:S(2)}, u32[]{:S(2)}) collective-permute-start(bf16[256,1024]{1,0:T(8,128)(2,1)} %shard_map.251), channel_id=1, source_target_pairs={{0,0},{1,7},{2,2},{3,5},{4,4},{5,3},{6,6},{7,1},{8,8},{9,15},{10,1... | collective-permute-start | bytes 1572872 | tf_op jit(solution)/shard_map/ppermute | solution.py:723
  420.4 11.2 %collective-permute-done.58 = bf16[256,1024]{1,0:T(8,128)(2,1)S(1)} collective-permute-done((bf16[256,1024]{1,0:T(8,128)(2,1)}, bf16[256,1024]{1,0:T(8,128)(2,1)S(1)}, u32[]{:S(2)}, u32[]{:S(2)}) %collective-permute-start.58) | collective-permute-done | bytes 524320 | tf_op jit(solution)/shard_map/ppermute | solution.py:723
  (351 shorter events, 188.9 us)
Async XLA Ops:
  7.2 107.0 %all-gather.5.cloned.1.call-start = ((), (), s32[]{:S(2)}) async-start(), calls=%async_computation.6 | async-start | bytes 3244032 | tf_op jit(solution)/shard_map/all_gather | solution.py:900
  39.9 142.0 %all-gather.7.cloned.1.call-start = ((), (), s32[]{:S(2)}) async-start(), calls=%async_computation.7 | async-start | bytes 5308416 | tf_op jit(solution)/shard_map/all_gather | solution.py:996
  70.1 27.8 %collective-permute-start.17 = (bf16[256,1024]{1,0:T(8,128)(2,1)}, bf16[256,1024]{1,0:T(8,128)(2,1)S(1)}, u32[]{:S(2)}, u32[]{:S(2)}) collective-permute-start(bf16[256,1024]{1,0:T(8,128)(2,1)} %param.25), channel_id=1, source_target_pairs={{0,0},{1,7},{2,2},{3,5},{4,4},{5,3},{6,6},{7,1},{8,8},{9,15},{10,1... | collective-permute-start | bytes 1572872 | tf_op jit(solution)/shard_map/ppermute | solution.py:723
  79.6 18.3 %collective-permute-start.16 = (bf16[2048,128]{1,0:T(8,128)(2,1)S(1)}, bf16[2048,128]{1,0:T(8,128)(2,1)}, u32[]{:S(2)}, u32[]{:S(2)}) collective-permute-start(bf16[2048,128]{1,0:T(8,128)(2,1)S(1)} %slice.143.kv_ref.refs_3_), channel_id=1, source_target_pairs={{0,2},{1,3},{2,4},{3,5},{4,6},{5,7},{6,0},{7,1},{8,10},{9,11},{10,... | collective-permute-start | bytes 1572872 | tf_op jit(solution)/shard_map/ppermute | solution.py:723
  113.7 213.7 %reduce-scatter.3.cloned.1.call-start = ((), (), s32[]{:S(2)}) async-start(), calls=%async_computation.4 | async-start | bytes 7962624 | tf_op jit(solution)/shard_map/reduce_scatter | solution.py:1058
  113.8 22.2 %collective-permute-start.21 = (bf16[2048,128]{1,0:T(8,128)(2,1)S(1)}, bf16[2048,128]{1,0:T(8,128)(2,1)}, u32[]{:S(2)}, u32[]{:S(2)}) collective-permute-start(bf16[2048,128]{1,0:T(8,128)(2,1)S(1)} %collective-permute-done.18.refs_2_.refs_3_), channel_id=1, source_target_pairs={{0,2},{1,3},{2,4},{3,5},{4,6},{5,7},{6,0},{7,1},{8,10},{9,11},{10,... | collective-permute-start | bytes 1572872 | tf_op jit(solution)/shard_map/ppermute | solution.py:723
  115.4 20.6 %collective-permute-start.25 = (bf16[256,1024]{1,0:T(8,128)(2,1)S(1)}, bf16[256,1024]{1,0:T(8,128)(2,1)S(1)}, u32[]{:S(2)}, u32[]{:S(2)}) collective-permute-start(bf16[256,1024]{1,0:T(8,128)(2,1)S(1)} %bitcast.120), channel_id=1, source_target_pairs={{0,16},{8,24},{16,0},{24,8},{1,17},{9,25},{17,1},{25,9},{2,18},{10... | collective-permute-start | bytes 1572872 | tf_op jit(solution)/shard_map/ppermute | solution.py:723
  115.8 20.2 %collective-permute-start.24 = (bf16[256,1024]{1,0:T(8,128)(2,1)S(1)}, bf16[256,1024]{1,0:T(8,128)(2,1)S(1)}, u32[]{:S(2)}, u32[]{:S(2)}) collective-permute-start(bf16[256,1024]{1,0:T(8,128)(2,1)S(1)} %bitcast.121), channel_id=1, source_target_pairs={{0,8},{8,0},{16,24},{24,16},{1,9},{9,1},{17,25},{25,17},{2,10},{10... | collective-permute-start | bytes 1572872 | tf_op jit(solution)/shard_map/ppermute | solution.py:723
  203.0 17.5 %collective-permute-start.33 = (bf16[256,1024]{1,0:T(8,128)(2,1)}, bf16[256,1024]{1,0:T(8,128)(2,1)S(1)}, u32[]{:S(2)}, u32[]{:S(2)}) collective-permute-start(bf16[256,1024]{1,0:T(8,128)(2,1)} %get-tuple-element.257), channel_id=1, source_target_pairs={{0,8},{8,0},{16,24},{24,16},{1,9},{9,1},{17,25},{25,17},{2,10},{10... | collective-permute-start | bytes 1572872 | tf_op jit(solution)/shard_map/ppermute | solution.py:723
  203.4 17.2 %collective-permute-start.34 = (bf16[256,1024]{1,0:T(8,128)(2,1)}, bf16[256,1024]{1,0:T(8,128)(2,1)S(1)}, u32[]{:S(2)}, u32[]{:S(2)}) collective-permute-start(bf16[256,1024]{1,0:T(8,128)(2,1)} %get-tuple-element.258), channel_id=1, source_target_pairs={{0,16},{8,24},{16,0},{24,8},{1,17},{9,25},{17,1},{25,9},{2,18},{10... | collective-permute-start | bytes 1572872 | tf_op jit(solution)/shard_map/ppermute | solution.py:723
  240.1 191.5 %reduce-scatter.5.cloned.1.call-start = ((), (), s32[]{:S(2)}) async-start(), calls=%async_computation.5 | async-start | bytes 2064384 | tf_op jit(solution)/shard_map/reduce_scatter | solution.py:1170
  240.6 35.9 %collective-permute-start.39 = (bf16[256,1024]{1,0:T(8,128)(2,1)}, bf16[256,1024]{1,0:T(8,128)(2,1)S(1)}, u32[]{:S(2)}, u32[]{:S(2)}) collective-permute-start(bf16[256,1024]{1,0:T(8,128)(2,1)} %get-tuple-element.285.refs_2_), channel_id=1, source_target_pairs={{0,16},{8,24},{16,0},{24,8},{1,17},{9,25},{17,1},{25,9},{2,18},{10... | collective-permute-start | bytes 1572872 | tf_op jit(solution)/shard_map/ppermute | solution.py:723
  242.0 34.4 %collective-permute-start.38 = (bf16[256,1024]{1,0:T(8,128)(2,1)}, bf16[256,1024]{1,0:T(8,128)(2,1)S(1)}, u32[]{:S(2)}, u32[]{:S(2)}) collective-permute-start(bf16[256,1024]{1,0:T(8,128)(2,1)} %get-tuple-element.285.refs_2_), channel_id=1, source_target_pairs={{0,8},{8,0},{16,24},{24,16},{1,9},{9,1},{17,25},{25,17},{2,10},{10... | collective-permute-start | bytes 1572872 | tf_op jit(solution)/shard_map/ppermute | solution.py:723
  276.5 20.2 %collective-permute-start.42 = (bf16[256,1024]{1,0:T(8,128)(2,1)}, bf16[256,1024]{1,0:T(8,128)(2,1)S(1)}, u32[]{:S(2)}, u32[]{:S(2)}) collective-permute-start(bf16[256,1024]{1,0:T(8,128)(2,1)} %get-tuple-element.297), channel_id=1, source_target_pairs={{0,8},{8,0},{16,24},{24,16},{1,9},{9,1},{17,25},{25,17},{2,10},{10... | collective-permute-start | bytes 1572872 | tf_op jit(solution)/shard_map/ppermute | solution.py:723
  277.7 18.9 %collective-permute-start.43 = (bf16[256,1024]{1,0:T(8,128)(2,1)}, bf16[256,1024]{1,0:T(8,128)(2,1)S(1)}, u32[]{:S(2)}, u32[]{:S(2)}) collective-permute-start(bf16[256,1024]{1,0:T(8,128)(2,1)} %get-tuple-element.298), channel_id=1, source_target_pairs={{0,16},{8,24},{16,0},{24,8},{1,17},{9,25},{17,1},{25,9},{2,18},{10... | collective-permute-start | bytes 1572872 | tf_op jit(solution)/shard_map/ppermute | solution.py:723
  277.9 18.8 %collective-permute-start.41 = (bf16[128,1024]{1,0:T(8,128)(2,1)S(1)}, bf16[128,1024]{1,0:T(8,128)(2,1)S(1)}, u32[]{:S(2)}, u32[]{:S(2)}) collective-permute-start(bf16[128,1024]{1,0:T(8,128)(2,1)S(1)} %slice.127), channel_id=1, source_target_pairs={{0,8},{8,0},{16,24},{24,16},{1,9},{9,1},{17,25},{25,17},{2,10},{10... | collective-permute-start | bytes 786440 | tf_op jit(solution)/shard_map/ppermute | solution.py:723
  279.3 17.3 %collective-permute-start.40 = (bf16[128,1024]{1,0:T(8,128)(2,1)S(1)}, bf16[128,1024]{1,0:T(8,128)(2,1)}, u32[]{:S(2)}, u32[]{:S(2)}) collective-permute-start(bf16[128,1024]{1,0:T(8,128)(2,1)S(1)} %slice.126), channel_id=1, source_target_pairs={{0,16},{8,24},{16,0},{24,8},{1,17},{9,25},{17,1},{25,9},{2,18},{10... | collective-permute-start | bytes 786440 | tf_op jit(solution)/shard_map/ppermute | solution.py:723
  297.4 19.8 %collective-permute-start.45 = (bf16[128,1024]{1,0:T(8,128)(2,1)S(1)}, bf16[128,1024]{1,0:T(8,128)(2,1)S(1)}, u32[]{:S(2)}, u32[]{:S(2)}) collective-permute-start(bf16[128,1024]{1,0:T(8,128)(2,1)S(1)} %add_convert_fusion.2), channel_id=1, source_target_pairs={{0,8},{8,0},{16,24},{24,16},{1,9},{9,1},{17,25},{25,17},{2,10},{10... | collective-permute-start | bytes 786440 | tf_op jit(solution)/shard_map/ppermute | solution.py:723
  298.7 18.4 %collective-permute-start.44 = (bf16[128,1024]{1,0:T(8,128)(2,1)S(1)}, bf16[128,1024]{1,0:T(8,128)(2,1)S(1)}, u32[]{:S(2)}, u32[]{:S(2)}) collective-permute-start(bf16[128,1024]{1,0:T(8,128)(2,1)S(1)} %add_convert_fusion.3), channel_id=1, source_target_pairs={{0,16},{8,24},{16,0},{24,8},{1,17},{9,25},{17,1},{25,9},{2,18},{10... | collective-permute-start | bytes 786440 | tf_op jit(solution)/shard_map/ppermute | solution.py:723
  299.0 49.3 %collective-permute-start.49 = (bf16[2048,128]{1,0:T(8,128)(2,1)}, bf16[2048,128]{1,0:T(8,128)(2,1)S(1)}, u32[]{:S(2)}, u32[]{:S(2)}) collective-permute-start(bf16[2048,128]{1,0:T(8,128)(2,1)} %get-tuple-element.327), channel_id=1, source_target_pairs={{0,6},{1,7},{2,0},{3,1},{4,2},{5,3},{6,4},{7,5},{8,14},{9,15},{10,... | collective-permute-start | bytes 1572872 | tf_op jit(solution)/shard_map/ppermute | solution.py:723
  316.9 31.4 %collective-permute-start.50 = (bf16[2048,128]{1,0:T(8,128)(2,1)}, bf16[2048,128]{1,0:T(8,128)(2,1)S(1)}, u32[]{:S(2)}, u32[]{:S(2)}) collective-permute-start(bf16[2048,128]{1,0:T(8,128)(2,1)} %get-tuple-element.328), channel_id=1, source_target_pairs={{0,2},{1,3},{2,4},{3,5},{4,6},{5,7},{6,0},{7,1},{8,10},{9,11},{10,... | collective-permute-start | bytes 1572872 | tf_op jit(solution)/shard_map/ppermute | solution.py:723
  317.2 32.0 %collective-permute-start.51 = (bf16[2048,128]{1,0:T(8,128)(2,1)}, bf16[2048,128]{1,0:T(8,128)(2,1)S(1)}, u32[]{:S(2)}, u32[]{:S(2)}) collective-permute-start(bf16[2048,128]{1,0:T(8,128)(2,1)} %get-tuple-element.329), channel_id=1, source_target_pairs={{0,4},{1,5},{2,6},{3,7},{4,0},{5,1},{6,2},{7,3},{8,12},{9,13},{10,... | collective-permute-start | bytes 1572872 | tf_op jit(solution)/shard_map/ppermute | solution.py:723
  402.2 18.2 %collective-permute-start.55 = (bf16[256,1024]{1,0:T(8,128)(2,1)}, bf16[256,1024]{1,0:T(8,128)(2,1)S(1)}, u32[]{:S(2)}, u32[]{:S(2)}) collective-permute-start(bf16[256,1024]{1,0:T(8,128)(2,1)} %shard_map.249), channel_id=1, source_target_pairs={{0,0},{1,7},{2,2},{3,5},{4,4},{5,3},{6,6},{7,1},{8,8},{9,15},{10,1... | collective-permute-start | bytes 1572872 | tf_op jit(solution)/shard_map/ppermute | solution.py:723
  412.0 19.7 %collective-permute-start.58 = (bf16[256,1024]{1,0:T(8,128)(2,1)}, bf16[256,1024]{1,0:T(8,128)(2,1)S(1)}, u32[]{:S(2)}, u32[]{:S(2)}) collective-permute-start(bf16[256,1024]{1,0:T(8,128)(2,1)} %shard_map.251), channel_id=1, source_target_pairs={{0,0},{1,7},{2,2},{3,5},{4,4},{5,3},{6,6},{7,1},{8,8},{9,15},{10,1... | collective-permute-start | bytes 1572872 | tf_op jit(solution)/shard_map/ppermute | solution.py:723
  (106 other events, 1039.5 us)
Sparse Core Ops, SparseCore 0:
  40.0 35.5 all-gather.4
  113.8 54.3 all-gather.6
  220.7 79.1 reduce-scatter.2
  373.8 32.3 reduce-scatter.4
